TPU v7x, 256 devices: a whole 4x4x8 slice. The times are simulated.
256 devices in a mesh: rep: 8 (over z_lo, core), fsdp: 32 (over z_hi, y, x).
Axes of the slice: x: 4, y: 4, z: 8 (z_hi: 2, z_lo: 4; z = z_hi * 4 + z_lo), core: 2. Of those that a mesh axis runs over, the one named last changes fastest.
Arguments:
- activations: bfloat16 [8, 24576, 6144], P('rep', 'fsdp'), may hold values from -6 to 6
- out_grads: bfloat16 [8, 24576, 512], P('rep', 'fsdp'), may hold values from -0.0390625 to 0.0390625
- momentum: float32 [8, 6144, 512], P('rep', 'fsdp'), may hold values from -6 to 6
- band: int32 [512], replicated, may hold values from 0 to 4095, as said below
Outputs:
- update: float32 [6144, 512], P('fsdp')
- new_momentum: float32 [8, 6144, 512], P('rep', 'fsdp')
Inputs may be any that keep to these rules, and one draw needn't show every extreme that they name: `band`: distinct positions in a group's flattened coefficients; 0 and 4095 are always among them.
All inputs are finite; a program needn't handle non-finite values.
Results may differ from a plain program's by a relative error of at most 0.0003.
Values may be sent and summed in bfloat16 or wider, within the bound.
No kernel may reach another device: no remote copies, remote signals or barrier semaphores. Data moves between devices by JAX's collectives and lax.ppermute only.
A program may use at most 128 MiB of HBM per device.

v0:
```python
import jax
import jax.numpy as jnp
from jax import lax
from jax.sharding import PartitionSpec as P

GROUP = 64


decay_rate = 0.999


def dct_table(order):
    steps = jnp.arange(order, dtype=jnp.float32)
    waves = jnp.cos(jnp.pi * (2.0 * steps[None, :] + 1.0) * steps[:, None] / (2.0 * order))
    waves = waves * jnp.sqrt(jnp.float32(2.0 / order))
    first = jnp.where(steps == 0, jnp.float32(0.5) ** 0.5, jnp.float32(1.0))
    return waves * first[:, None]


def to_coeffs(matrix, table, blockdiag):
    rows, width = matrix.shape
    order = table.shape[0]
    left = jnp.einsum(
        "ij,rjk->rik",
        table,
        matrix.reshape(rows // order, order, width),
        precision=lax.Precision.HIGHEST,
    )
    both = jnp.dot(left.reshape(rows, width), blockdiag.T, precision=lax.Precision.HIGHEST)
    blocks = both.reshape(rows // order, order, width // order, order).transpose(0, 2, 1, 3)
    return blocks.reshape(rows // order, width // order, order * order)


def from_band(values, band, table, blockdiag):
    order = table.shape[0]
    lead = values.shape[:-3]
    row_blocks, col_blocks = (values.shape[-3], values.shape[-2])
    full = (
        jnp.zeros(lead + (row_blocks, col_blocks, order * order), jnp.float32)
        .at[..., band]
        .set(values)
    )
    blocks = full.reshape(lead + (row_blocks, col_blocks, order, order))
    blocks = jnp.moveaxis(blocks, -2, -3).reshape(lead + (row_blocks, order, col_blocks * order))
    left = jnp.einsum("ji,...rjk->...rik", table, blocks, precision=lax.Precision.HIGHEST)
    flat = left.reshape(lead + (row_blocks * order, col_blocks * order))
    return jnp.matmul(flat, blockdiag, precision=lax.Precision.HIGHEST)


def shards(activations, out_grads, momentum, band):
    acts = activations[0]
    grad_out = out_grads[0]
    width = momentum.shape[2]
    contract = (((0,), (0,)), ((), ()))
    grad = lax.psum_scatter(
        lax.dot_general(acts, grad_out, contract, preferred_element_type=jnp.float32),
        "fsdp",
        scatter_dimension=0,
        tiled=True,
    )
    table = dct_table(GROUP)
    blockdiag = jnp.kron(jnp.eye(width // GROUP, dtype=jnp.float32), table)
    mom_now = decay_rate * momentum[0] + grad
    kept = to_coeffs(mom_now, table, blockdiag)[:, :, band]
    every_band = lax.all_gather(kept[None], "rep", axis=0, tiled=True)
    summed_band = jnp.sum(every_band, axis=0)
    shared = summed_band / lax.axis_size("rep")
    both_back = from_band(jnp.stack([shared, kept]), band, table, blockdiag)
    update = both_back[0]
    new_momentum = mom_now - both_back[1]
    return (update, new_momentum[None])


def solution(mesh):
    return jax.shard_map(
        shards,
        mesh=mesh,
        in_specs=(P("rep", "fsdp", None), P("rep", "fsdp", None), P("rep", "fsdp", None), P()),
        out_specs=(P("fsdp", None), P("rep", "fsdp", None)),
        check_vma=False,
    )
```

profile of v0, /device:TPU:1, one launch (start us, length us, event | category | flops | bytes accessed | tf_op | source)
XLA Modules:
  0.0 447.0 jit_solution(5892907463540333814)
XLA Ops:
  7.2 0.0 copy-start
  7.2 0.0 reduce-scatter.2.cloned.1.call-start
  7.2 1.1 copy-done
  8.3 11.8 %fusion = f32[6144,512]{1,0:T(8,128)} fusion(bf16[1,768,6144]{2,1,0:T(8,128)(2,1)} %param.4, bf16[1,768,512]{2,1,0:T(8,128)(2,1)S(1)} %copy-done), kind=kOutput, calls=%fused_computation.2 | convolution fusion | flops 4831838208 | bytes 22806528 | tf_op jit(solution)/shard_map/dot_general | solution.py:56
  20.1 0.0 copy-start.4
  20.1 0.0 copy-start.3
  20.1 0.0 reduce-scatter.2.cloned.1.call-update
  20.2 0.2 cosine_multiply_fusion
  20.4 0.1 copy.17
  20.5 0.1 mul.179
  20.6 0.1 mul.175
  20.7 0.1 mul.176
  20.8 0.2 broadcast_multiply_fusion
  21.0 1.5 reshape.138
  22.5 0.0 copy-done.4
  22.5 306.8 %reduce-scatter.2.cloned.1.call-done = f32[192,512]{1,0:T(8,128)} async-done(((f32[6144,512]{1,0:T(8,128)}), f32[192,512]{1,0:T(8,128)}) %reduce-scatter.2.cloned.1.call-update) | async-done | bytes 393232 | tf_op jit(solution)/shard_map/reduce_scatter | solution.py:55
  329.3 0.0 copy-done.3
  329.3 1.1 bitcast_add_fusion
  330.3 0.0 copy-start.2
  330.3 0.7 copy-done.2
  331.1 0.7 convolution_bitcast_fusion.1
  331.8 1.4 convolution_bitcast_fusion
  333.2 5.9 %copy.28 = f32[3,8,64,64]{1,0,3,2:T(4,128)} copy(f32[3,8,64,64]{3,2,1,0:T(8,128)S(1)} %convolution_bitcast_fusion) | data formatting | bytes 786432 | tf_op jit(solution)/shard_map/reshape | solution.py:31
  339.1 4.9 %gather_fusion = f32[512,3,8]{2,1,0:T(4,128)S(1)} fusion(f32[3,8,4096]{1,0,2:T(4,128)} %bitcast.62, s32[1024]{0:T(1024)S(1)} %pad_clamp_fusion), kind=kCustom, calls=%fused_computation | custom fusion | bytes 100352 | tf_op jit(solution)/shard_map/gather | solution.py:64
  344.0 0.3 copy.19
  344.2 16.8 %all-gather = f32[24,8,512]{2,1,0:T(8,128)S(1)} all-gather(f32[3,8,512]{2,1,0:T(8,128)S(1)} %copy.19), channel_id=2, replica_groups=mesh['rep'=8,'fsdp'=32] {'rep'}, dimensions={0}, use_global_device_ids=true | all-gather | bytes 442368 | tf_op jit(solution)/shard_map/all_gather | solution.py:65
  361.1 1.1 copy.21
  362.2 4.9 %broadcast_in_dim.26 = f32[2,3,8,4096]{2,0,3,1:T(2,128)} broadcast(f32[]{:T(128)} %constant.11.clone.1), dimensions={} | broadcast | bytes 786436 | tf_op jit(solution)/shard_map/broadcast_in_dim | solution.py:39
  367.0 0.0 copy-start.1
  367.1 52.9 %scatter_fusion = f32[2,3,8,4096]{2,0,3,1:T(2,128)} fusion(f32[2,3,8,4096]{2,0,3,1:T(2,128)} %broadcast_in_dim.26, s32[512]{0:T(512)S(1)} %compare_select_fusion, f32[512,2,3,8]{3,1,2,0:T(2,128)S(1)} %copy.21), kind=kCustom, calls=%fused_computation.1 | custom fusion | bytes 296960 | tf_op jit(solution)/shard_map/scatter | solution.py:41
  419.9 12.8 %copy.22 = f32[2,3,64,8,64]{4,3,2,1,0:T(8,128)S(1)} copy(f32[2,3,64,8,64]{3,0,4,2,1:T(2,128)} %bitcast.61) | data formatting | bytes 1572864 | tf_op jit(solution)/shard_map/transpose | solution.py:44
  432.7 1.3 reshape.113
  434.0 2.2 fusion.9
  436.2 0.0 copy-done.1
  436.2 1.4 fusion.22
  437.6 1.8 fusion.8
  439.4 0.8 slice_bitcast_fusion.1
  (8 shorter events, 0.1 us)
Async XLA Ops:
  7.2 1.1 copy-start
  7.2 322.1 %reduce-scatter.2.cloned.1.call-start = ((), (), s32[]{:S(2)}) async-start(), calls=%async_computation.1 | async-start | bytes 12976128 | tf_op jit(solution)/shard_map/reduce_scatter | solution.py:55
  20.1 2.4 copy-start.4
  20.1 309.1 %copy-start.3 = (f32[1,192,512]{2,1,0:T(8,128)S(1)}, f32[1,192,512]{2,1,0:T(8,128)}, u32[]{:S(2)}) copy-start(f32[1,192,512]{2,1,0:T(8,128)} %param.6) | copy-start | bytes 1179652
  330.3 0.7 copy-start.2
  367.0 69.1 %copy-start.1 = (f32[512,512,1]{1,0,2:T(8,128)S(1)}, f32[512,512,1]{1,0,2:T(8,128)}, u32[]{:S(2)}) copy-start(f32[512,512,1]{1,0,2:T(8,128)} %reshape.138) | copy-start | bytes 3145732
Sparse Core Ops, SparseCore 0:
  20.3 308.9 reduce-scatter.1
where the time goes:
time: 449 us; the launch traced here: 447 us
  waiting for transfers between devices  307 us (68%)
  local copies, waits for them, and re-layouts  88.4 us (20%)
  matrix products  17.6 us (4%)
  blocking collectives  16.8 us (4%)
  between operations  14.2 us (3%)
    reduce_scatter x1, waiting for transfers between devices, shards(): lax.psum_scatter(lax.dot_general(acts, grad_out, contract, preferred_elem...  307 us
    scatter x1, local copies, waits for them, and re-layouts, from_band(): full = jnp.zeros(lead + (row_blocks, col_blocks, order * order), jnp.floa...  52.9 us
    all_gather x1, blocking collectives, shards(): every_band = lax.all_gather(kept[None], 'rep', axis=0, tiled=True)  16.8 us
    transpose x1, local copies, waits for them, and re-layouts, from_band(): jnp.moveaxis(blocks, -2, -3)  12.8 us
    dot_general x1, matrix products, shards(): lax.dot_general(acts, grad_out, contract, preferred_element_type=jnp.floa...  11.8 us
  transfers between devices with their start and end apart: 1, of which 1 were waited for; matrix products, arithmetic and copies ran while one was open for 1% of the time, Pallas kernels for 0%

commit v1 on v0

v1 whole, which is shorter than its diff:
```python
import functools

import jax
import jax.numpy as jnp
import numpy as np
from jax import lax
from jax.experimental import pallas as pl
from jax.experimental.pallas import tpu as pltpu
from jax.sharding import PartitionSpec as P

GROUP = 64
REPS = 8
DECAY = 0.999
HEAD = 16
STEPS = 256.0
TOP = 32766.0
LIMIT = 56 << 20
F32 = jnp.float32
I16 = jnp.int16
BF16 = jnp.bfloat16
CHAINS = ((1, 3), (3, 1))


def dct_table(order):
    n = np.arange(order)
    table = np.cos(np.pi * (2 * n[None, :] + 1) * n[:, None] / (2 * order)) * np.sqrt(2.0 / order)
    table[0] *= np.sqrt(0.5)
    return table.astype(np.float32)


def scale_code(biggest):
    top = jnp.max(biggest, axis=0, keepdims=True)
    return jnp.ceil(jnp.log2(jnp.maximum(top, 2.0**-110)) * STEPS)


def column_peak(x):
    return jnp.max(jnp.abs(x).reshape(x.shape[0] // 8, 8, x.shape[1]), axis=0)


def put_head(out, code):
    rows = jnp.broadcast_to(code, (HEAD, code.shape[1]))
    out[:HEAD, :] = rows.astype(jnp.int32).astype(I16)


def quantise(x, code):
    return jnp.round(x * (TOP * jnp.exp2(code * (-1.0 / STEPS)))).astype(jnp.int32).astype(I16)


def scale_of(msg):
    code = msg[:HEAD, :].astype(jnp.int32).astype(F32)[:1]
    return jnp.exp2(code * (1.0 / STEPS)) * (1.0 / TOP)


def dequantise(msg, block, rows, scale):
    return msg[HEAD + block * rows : HEAD + (block + 1) * rows, :].astype(jnp.int32).astype(F32) * scale


def partial_kernel(outs, late, passed, tabs, acts, og, *rest):
    n = len(outs)
    tab = tabs.at[late]
    rest = rest[passed:]
    out_refs = rest[:n]
    pieces, acc, peak, ready, in_sems, out_sems = rest[n + passed :]
    count, rows, half = acc.shape[2:]

    def fetch(i):
        first = pl.multiple_of(tab[0, i] * 2 * rows, 128)
        return pltpu.make_async_copy(acts.at[:, pl.ds(first, 2 * rows)], pieces.at[i], in_sems.at[i])

    for i in range(count):
        fetch(i).start()
    peak[...] = jnp.zeros_like(peak)

    @pl.loop(0, count)
    def _(i):
        fetch(i).wait()
        both = lax.dot_general(
            pieces[i], og[...], (((0,), (0,)), ((), ())), preferred_element_type=F32
        )
        for s in range(2):
            slot = tab[1 + s, i]
            part = both[s * rows : (s + 1) * rows]
            peak[slot] = jnp.maximum(peak[slot], column_peak(part))
            for c in range(2):
                place = tab[3 + 2 * c + s, i]
                acc[c, slot, place] = part[:, c * half : (c + 1) * half]
                for k, (k_slot, k_c, kind) in enumerate(outs):
                    if kind == "f" and k_c == c:

                        @pl.when(slot == k_slot)
                        def _():
                            pltpu.make_async_copy(
                                acc.at[c, k_slot, place], out_refs[k].at[place], out_sems.at[k]
                            ).start()

    copies = []
    for k, (slot, c, kind) in enumerate(outs):
        if kind == "f":
            copies.append(pltpu.make_async_copy(acc.at[c, slot], out_refs[k], out_sems.at[k]))
    q = 0
    for k, (slot, c, kind) in enumerate(outs):
        if kind == "q":
            out = ready.at[q]
            code = scale_code(peak[slot][:, c * half : (c + 1) * half])
            put_head(out, code)
            for b in range(count):
                out[HEAD + b * rows : HEAD + (b + 1) * rows, :] = quantise(acc[c, slot, b], code)
            copies.append(pltpu.make_async_copy(out, out_refs[k], out_sems.at[k]))
            copies[-1].start()
            q += 1
    for copy in copies:
        copy.wait()


def partials(outs, late, tab, acts, og, rows, through=()):
    tokens, _ = acts.shape
    width = og.shape[1]
    half = width // 2
    count = tab.shape[2]
    shapes = [
        jax.ShapeDtypeStruct((HEAD + count * rows, half), I16) if kind == "q" else f32(count, rows, half)
        for _, _, kind in outs
    ]
    messages = sum(kind == "q" for _, _, kind in outs)
    anywhere = pl.BlockSpec(memory_space=pl.ANY)
    return pl.pallas_call(
        functools.partial(partial_kernel, outs, late, len(through)),
        in_specs=[pl.BlockSpec(memory_space=pltpu.SMEM), anywhere, pl.BlockSpec(memory_space=pltpu.VMEM)]
        + [anywhere] * len(through),
        out_specs=[anywhere] * (len(outs) + len(through)),
        out_shape=shapes + [jax.ShapeDtypeStruct(t.shape, t.dtype) for t in through],
        input_output_aliases={3 + k: len(outs) + k for k in range(len(through))},
        scratch_shapes=[
            pltpu.VMEM((count, tokens, 2 * rows), BF16),
            pltpu.VMEM((2, 2, count, rows, half), F32),
            pltpu.VMEM((2, 8, width), F32),
            pltpu.VMEM((messages, HEAD + count * rows, half), I16),
            pltpu.SemaphoreType.DMA((count,)),
            pltpu.SemaphoreType.DMA((len(outs),)),
        ],
        compiler_params=pltpu.CompilerParams(vmem_limit_bytes=LIMIT),
        cost_estimate=pl.CostEstimate(
            flops=2 * tokens * count * 2 * rows * width, bytes_accessed=tokens * count * 2 * rows * 2, transcendentals=0
        ),
    )(tab, acts, og, *through)


def whole(shape, index=None):
    return pl.BlockSpec(shape, lambda i: index or (0,) * len(shape))


def call(kernel, ins, in_specs, outs, scratch=(), limit=16 << 20):
    total = sum(x.size * x.dtype.itemsize for x in ins) + sum(np.prod(o.shape) * o.dtype.itemsize for o in outs)
    return pl.pallas_call(
        kernel,
        grid=(1,),
        in_specs=in_specs,
        out_specs=[whole(o.shape) for o in outs],
        out_shape=outs,
        scratch_shapes=list(scratch),
        compiler_params=pltpu.CompilerParams(vmem_limit_bytes=limit),
        cost_estimate=pl.CostEstimate(flops=4 * int(total), bytes_accessed=int(total), transcendentals=0),
    )(*ins)


def i16(rows, width):
    return jax.ShapeDtypeStruct((HEAD + rows, width), I16)


def f32(*shape):
    return jax.ShapeDtypeStruct(shape, F32)


def second_kernel(own, first, out_a, out_b, held):
    rows = own.shape[1]
    quarter = own.shape[0] // 2
    scale = scale_of(first)
    for out, start in ((out_a, 0), (out_b, quarter)):
        peak = None
        for b in range(quarter):
            x = own[start + b] + dequantise(first, start + b, rows, scale)
            held[b] = x
            p = column_peak(x)
            peak = p if peak is None else jnp.maximum(peak, p)
        code = scale_code(peak)
        put_head(out, code)
        for b in range(quarter):
            out[HEAD + b * rows : HEAD + (b + 1) * rows, :] = quantise(held[b], code)


def third_kernel(own, near, far, out, held):
    rows = own.shape[1]
    n = own.shape[0]
    scale_n, scale_f = scale_of(near), scale_of(far)
    peak = None
    for b in range(n):
        x = own[b] + dequantise(near, b, rows, scale_n) + dequantise(far, b, rows, scale_f)
        held[b] = x
        p = column_peak(x)
        peak = p if peak is None else jnp.maximum(peak, p)
    code = scale_code(peak)
    put_head(out, code)
    for b in range(n):
        out[HEAD + b * rows : HEAD + (b + 1) * rows, :] = quantise(held[b], code)


def fourth_kernel(own, near, far, third, out, keep, held):
    rows = own.shape[1]
    n = own.shape[0]
    scale_n, scale_f, scale_t = scale_of(near), scale_of(far), scale_of(third)
    peak = None
    for b in range(n):
        x = own[b] + dequantise(near, n + b, rows, scale_n) + dequantise(far, b, rows, scale_f)
        x = x + dequantise(third, b, rows, scale_t)
        if b < n // 2:
            held[b] = x
            p = column_peak(x)
            peak = p if peak is None else jnp.maximum(peak, p)
        else:
            keep[b - n // 2] = x
    code = scale_code(peak)
    put_head(out, code)
    for b in range(n // 2):
        out[HEAD + b * rows : HEAD + (b + 1) * rows, :] = quantise(held[b], code)


def fifth_kernel(keep0, keep1, msg0, msg1, out, mine):
    rows = keep0.shape[1]
    half = keep0.shape[2]
    for c, (keep, msg) in enumerate(((keep0, msg0), (keep1, msg1))):
        cols = slice(c * half, (c + 1) * half)
        scale = scale_of(msg)
        mine[:, cols] = keep[0] + dequantise(msg, 0, rows, scale)
        x = keep[1] + dequantise(msg, 1, rows, scale)
        code = scale_code(column_peak(x))
        out[:HEAD, cols] = jnp.broadcast_to(code, (HEAD, half)).astype(jnp.int32).astype(I16)
        out[HEAD:, cols] = quantise(x, code)


def split(x):
    high = x.astype(BF16)
    return high, (x - high.astype(F32)).astype(BF16)


def mm(a, b):
    return jnp.dot(a, b, preferred_element_type=F32)


def waves_kernel(band, table, wa, wh, wl, th, tl):
    order = table.shape[0]
    n = band.shape[1]
    t = table[...]
    t0 = t.astype(BF16)
    r = t - t0.astype(F32)
    t1 = r.astype(BF16)
    t2 = (r - t1.astype(F32)).astype(BF16)
    ids = lax.broadcasted_iota(jnp.int32, (order, n), 0)
    pos = jnp.broadcast_to(band[...], (order, n))

    def pick(which):
        hot = jnp.where(ids == which, 1.0, 0.0).astype(BF16)
        return mm(t0, hot) + mm(t1, hot) + mm(t2, hot)

    left = pick(lax.shift_right_logical(pos, 6))
    right = pick(jnp.bitwise_and(pos, order - 1))
    for g in range(wa.shape[0] // order):
        wa[g * order : (g + 1) * order, :] = left
    high, low = split(right)
    for out, back, x in ((wh, th, high), (wl, tl, low)):
        x = x.astype(F32)
        zero = jnp.zeros_like(x)
        both = jnp.concatenate(
            [jnp.concatenate([x, zero], axis=1), jnp.concatenate([zero, x], axis=1)], axis=0
        )
        out[...] = both.astype(BF16)
        back[...] = both.T.astype(BF16)


def kept_kernel(mine, msg, momentum, wa, wh, wl, mom, kept):
    rows, width = mine.shape
    n = wa.shape[1]
    pairs = width // 128
    grad = mine[...] + msg[HEAD:, :].astype(jnp.int32).astype(F32) * scale_of(msg)
    now = DECAY * momentum[...] + grad
    mom[...] = now
    left = wa[...]
    for p in range(pairs):
        high, low = split(now[:, p * 128 : (p + 1) * 128])
        y = mm(high, wh[...]) + mm(low, wh[...]) + mm(high, wl[...])
        for h in range(2):
            z = left * y[:, h * n : (h + 1) * n]
            for g in range(rows // GROUP):
                row = g * 2 * pairs + 2 * p + h
                kept[row : row + 1, :] = jnp.sum(z[g * GROUP : (g + 1) * GROUP], axis=0, keepdims=True)


def back(values, wa, th, tl, store):
    n = wa.shape[1]
    groups = wa.shape[0] // GROUP
    pairs = values.shape[0] // groups // 2
    left = wa[:GROUP, :]
    for p in range(pairs):
        stacked = []
        for g in range(groups):
            row = g * 2 * pairs + 2 * p
            stacked.append(
                jnp.concatenate([left * values[row : row + 1], left * values[row + 1 : row + 2]], axis=1)
            )
        high, low = split(jnp.concatenate(stacked, axis=0))
        store(p, mm(high, th[...]) + mm(low, th[...]) + mm(high, tl[...]))


def momentum_kernel(mom, kept, wa, th, tl, out):
    def store(p, x):
        cols = slice(p * 128, (p + 1) * 128)
        out[:, cols] = mom[:, cols] - x

    back(kept[...], wa, th, tl, store)


def update_kernel(total, wa, th, tl, out):
    def store(p, x):
        out[:, p * 128 : (p + 1) * 128] = x

    back(total[...] * (1.0 / REPS), wa, th, tl, store)


def coords(f):
    return f // 16, (f // 4) % 4, f % 4


def partner_pairs(chain_step, late):
    pairs = []
    for rep in range(8):
        core = rep % 2
        for f in range(32):
            z, y, x = coords(f)
            if (core == 0) != late:
                x ^= chain_step
            else:
                y ^= chain_step
            pairs.append((rep * 32 + f, rep * 32 + z * 16 + y * 4 + x))
    return pairs


def far_pairs():
    return [(rep * 32 + f, rep * 32 + (f ^ 16)) for rep in range(8) for f in range(32)]


ORDERS = tuple((2, m1, m2, 0) for m1, m2 in CHAINS)


def tables():
    found = np.zeros((2, 32, 2, 7, 8), np.int32)
    for core in range(2):
        for f in range(32):
            z, y, x = coords(f)
            u, v = (x, y) if core == 0 else (y, x)
            for late in range(2):
                far_half = (u >> 1) ^ (1 - late)
                for i in range(8):
                    zr, a, b = i // 4, (i // 2) % 2, i % 2
                    yd, xh = (2 * a + b, far_half) if core == 0 else (2 * far_half + a, b)
                    column = [(z ^ zr) * 8 + yd * 2 + xh]
                    both = [((2 * xh + s, yd) if core == 0 else (yd, 2 * xh + s)) for s in range(2)]
                    column += [(ud ^ u) & 1 for ud, _ in both]
                    for order in ORDERS:
                        column += [order.index(vd ^ v) * 2 + zr for _, vd in both]
                    found[core, f, late, :, i] = column
    return found.reshape(64, 2, 7, 8)


def shards(activations, out_grads, momentum, band):
    acts, og, momentum = activations[0], out_grads[0], momentum[0]
    rows, width = momentum.shape
    half = width // 2
    axes = ("rep", "fsdp")
    core = lax.axis_index("rep") % 2
    place = core * 32 + lax.axis_index("fsdp")
    tab = lax.dynamic_index_in_dim(jnp.asarray(tables()), place, keepdims=False)

    table = jnp.asarray(dct_table(GROUP).T)
    n = band.shape[0]
    wa, wh, wl, th, tl = call(
        waves_kernel,
        (band.reshape(1, n), table),
        [whole((1, n)), whole((GROUP, GROUP))],
        [f32(rows, n)]
        + [jax.ShapeDtypeStruct((128, 2 * n), BF16)] * 2
        + [jax.ShapeDtypeStruct((2 * n, 128), BF16)] * 2,
    )

    def swap(x, step, late):
        return lax.ppermute(x, axes, partner_pairs(step, late))

    m1a0, m1a1, m1b1, own0 = partials(((0, 0, "q"), (0, 1, "q"), (1, 1, "q"), (1, 0, "f")), 0, tab, acts, og, rows)
    r1a = [swap(m1a0, CHAINS[0][0], False), swap(m1a1, CHAINS[1][0], False)]
    m1b0, own1, keep0, keep1, m1b1 = partials(
        ((1, 0, "q"), (1, 1, "f"), (0, 0, "f"), (0, 1, "f")), 1, tab, acts, og, rows, (m1b1,)
    )
    r1b = [swap(m1b0, CHAINS[0][0], False), swap(m1b1, CHAINS[1][0], False)]
    own, keep = [own0, own1], [keep0, keep1]

    msg8, msg4, msg2 = i16(8 * rows, half), i16(4 * rows, half), i16(2 * rows, half)
    four = (4, rows, half)
    kept4, r4 = [], []
    r2, r3 = [], []
    for c, (m1, m2) in enumerate(CHAINS):
        m2a, m2b = call(
            second_kernel,
            (own[c], r1a[c]),
            [whole((8, rows, half)), whole(msg8.shape)],
            [msg4, msg4],
            [pltpu.VMEM(four, F32)],
        )
        r2.append((swap(m2a, m2, False), swap(m2b, m2, False)))
    for c, (m1, m2) in enumerate(CHAINS):
        (m3,) = call(
            third_kernel,
            (keep[c], r1b[c], r2[c][0]),
            [whole(four), whole(msg4.shape), whole(msg4.shape)],
            [msg4],
            [pltpu.VMEM(four, F32)],
        )
        r3.append(swap(m3, m1, True))
    for c, (m1, m2) in enumerate(CHAINS):
        m4, k4 = call(
            fourth_kernel,
            (keep[c], r1b[c], r2[c][1], r3[c]),
            [whole(four, (1, 0, 0)), whole(msg8.shape), whole(msg4.shape), whole(msg4.shape)],
            [msg2, f32(2, rows, half)],
            [pltpu.VMEM((2, rows, half), F32)],
        )
        kept4.append(k4)
        r4.append(swap(m4, m2, True))
    m5, mine = call(
        fifth_kernel,
        (*kept4, *r4),
        [whole((2, rows, half))] * 2 + [whole(msg2.shape)] * 2,
        [i16(rows, width), f32(rows, width)],
    )
    r5 = lax.ppermute(m5, axes, far_pairs())
    groups = (rows // GROUP) * (width // GROUP)
    mom, kept = call(
        kept_kernel,
        (mine, r5, momentum, wa, wh, wl),
        [whole(a.shape) for a in (mine, r5, momentum, wa, wh, wl)],
        [f32(rows, width), f32(groups, n)],
    )
    total = kept
    for bit in (1, 2, 4):
        total = total + lax.ppermute(total, "rep", [(r, r ^ bit) for r in range(REPS)])
    (new_momentum,) = call(
        momentum_kernel,
        (mom, kept, wa, th, tl),
        [whole(a.shape) for a in (mom, kept, wa, th, tl)],
        [f32(rows, width)],
    )
    (update,) = call(
        update_kernel,
        (total, wa, th, tl),
        [whole(a.shape) for a in (total, wa, th, tl)],
        [f32(rows, width)],
    )
    return update, new_momentum[None]


def solution(mesh):
    return jax.shard_map(
        shards,
        mesh=mesh,
        in_specs=(P("rep", "fsdp", None), P("rep", "fsdp", None), P("rep", "fsdp", None), P()),
        out_specs=(P("fsdp", None), P("rep", "fsdp", None)),
        check_vma=False,
    )
```

time: 449 us -> 87.2 us (0.19)
  waiting for transfers between devices: 307 us -> 26.7 us
  local copies, waits for them, and re-layouts: 88.4 us -> 1.34 us
  starting transfers between devices: 0.04 us -> 33.7 us
  Pallas kernels: 0 us -> 24.5 us
  matrix products: 17.6 us -> 0 us
  blocking collectives: 16.8 us -> 0 us
  between operations: 14.2 us -> 0.82 us
    reduce_scatter x1 -> x0, waiting for transfers between devices: 307 us -> none  [shards(): lax.psum_scatter(lax.dot_general(acts, grad_out, contract, preferred_elem...]
    scatter x1 -> x0, local copies, waits for them, and re-layouts: 52.9 us -> none  [from_band(): full = jnp.zeros(lead + (row_blocks, col_blocks, order * order), jnp.floa...]
    ppermute x0 -> x16, starting transfers between devices: none -> 33.7 us  [the longest x12 17.2 us: swap(): return lax.ppermute(x, axes, partner_pairs(step, late))]
    ppermute x0 -> x16, waiting for transfers between devices: none -> 26.7 us  [the longest x12 20 us: swap(): return lax.ppermute(x, axes, partner_pairs(step, late))]
    pallas_call x0 -> x13, Pallas kernels: none -> 24.5 us  [the longest x2 15.7 us: partials(): pl.pallas_call(functools.partial(partial_kernel, outs, late, len(through)...]
    dot_general x5 -> x0, matrix products: 17.6 us -> none  [the longest x1 11.8 us: shards(): lax.dot_general(acts, grad_out, contract, preferred_element_type=jnp.floa...]
    all_gather x1 -> x0, blocking collectives: 16.8 us -> none  [shards(): every_band = lax.all_gather(kept[None], 'rep', axis=0, tiled=True)]
    transpose x1 -> x0, local copies, waits for them, and re-layouts: 12.8 us -> none  [from_band(): jnp.moveaxis(blocks, -2, -3)]
  transfers between devices with their start and end apart: 1 -> 16, of which waited for: 1 -> 8; matrix products, arithmetic and copies ran while one was open for 1% -> 0% of each run, Pallas kernels for 0% -> 14%
where the time goes in v1:
time: 87.2 us; the launch traced here: 87 us
  starting transfers between devices  33.7 us (39%)
  waiting for transfers between devices  26.7 us (31%)
  Pallas kernels  24.5 us (28%)
  local copies, waits for them, and re-layouts  1.34 us (2%)
    ppermute x12, waiting for transfers between devices, swap(): return lax.ppermute(x, axes, partner_pairs(step, late))  20 us
    ppermute x12, starting transfers between devices, swap(): return lax.ppermute(x, axes, partner_pairs(step, late))  17.2 us
    pallas_call x2, Pallas kernels, partials(): pl.pallas_call(functools.partial(partial_kernel, outs, late, len(through)...  15.7 us
    ppermute x3, starting transfers between devices, shards(): lax.ppermute(total, 'rep', [(r, r ^ bit) for r in range(REPS)])  9.25 us
    pallas_call x11, Pallas kernels, call(): pl.pallas_call(kernel, grid=(1,), in_specs=in_specs, out_specs=[whole(o.s...  8.78 us
    ppermute x1, starting transfers between devices, shards(): r5 = lax.ppermute(m5, axes, far_pairs())  7.24 us
    ppermute x3, waiting for transfers between devices, shards(): lax.ppermute(total, 'rep', [(r, r ^ bit) for r in range(REPS)])  3.81 us
    ppermute x1, waiting for transfers between devices, shards(): r5 = lax.ppermute(m5, axes, far_pairs())  2.88 us
  transfers between devices with their start and end apart: 16, of which 8 were waited for; matrix products, arithmetic and copies ran while one was open for 0% of the time, Pallas kernels for 14%

profile of v1, /device:TPU:1, one launch (start us, length us, event | category | flops | bytes accessed | tf_op | source)
XLA Modules:
  0.0 87.0 jit_solution(7913554333851347138)
XLA Ops:
  0.6 0.7 dynamic-slice_bitcast_fusion
  1.3 0.6 copy.10.tabs
  2.0 8.1 %shard_map.77 = (s16[1552,256]{1,0:T(8,128)(2,1)}, s16[1552,256]{1,0:T(8,128)(2,1)}, s16[1552,256]{1,0:T(8,128)(2,1)}, f32[8,192,256]{2,1,0:T(8,128)}) custom-call(s32[2,7,8]{2,1,0:T(8,128)} %copy.10.tabs, bf16[768,6144]{1,0:T(8,128)(2,1)} %bitcast.9, bf16[768,512]{1,0:T(8,128)(2,1)} %bitcast.11), custom_call_target="tpu_custom_call" | custom-call | flops 2415919104 | bytes 4718592 | tf_op jit(solution)/shard_map/pallas_call | solution.py:126
  10.0 2.2 %collective-permute-start.1 = (s16[1552,256]{1,0:T(8,128)(2,1)}, s16[1552,256]{1,0:T(8,128)(2,1)S(1)}, u32[]{:S(2)}, u32[]{:S(2)}) collective-permute-start(s16[1552,256]{1,0:T(8,128)(2,1)} %get-tuple-element.32), channel_id=1, source_target_pairs={{0,1},{1,0},{2,3},{3,2},{4,5},{5,4},{6,7},{7,6},{8,9},{9,8},{10,11... | collective-permute-start | bytes 2383880 | tf_op jit(solution)/shard_map/ppermute | solution.py:394
  12.2 1.9 %collective-permute-start.6 = (s16[1552,256]{1,0:T(8,128)(2,1)}, s16[1552,256]{1,0:T(8,128)(2,1)S(1)}, u32[]{:S(2)}, u32[]{:S(2)}) collective-permute-start(s16[1552,256]{1,0:T(8,128)(2,1)} %get-tuple-element.39), channel_id=1, source_target_pairs={{0,3},{1,2},{2,1},{3,0},{4,7},{5,6},{6,5},{7,4},{8,11},{9,10},{10,... | collective-permute-start | bytes 2383880 | tf_op jit(solution)/shard_map/ppermute | solution.py:394
  14.1 7.6 %shard_map.78 = (s16[1552,256]{1,0:T(8,128)(2,1)}, f32[8,192,256]{2,1,0:T(8,128)}, f32[8,192,256]{2,1,0:T(8,128)}, f32[8,192,256]{2,1,0:T(8,128)}, s16[1552,256]{1,0:T(8,128)(2,1)}) custom-call(s32[2,7,8]{2,1,0:T(8,128)} %copy.10.tabs, bf16[768,6144]{1,0:T(8,128)(2,1)} %bitcast.10, bf16[768,512]{1,0:T(8,128)(2,1)} %bitcast.12, ...), custom_call_target="tpu_custom_call", output_to_operand_aliasing={{4}: (3, {})} | custom-call | flops 2415919104 | bytes 4718592 | tf_op jit(solution)/shard_map/pallas_call | solution.py:126
  21.8 0.5 collective-permute-start
  22.3 0.6 collective-permute-start.5
  22.9 0.0 collective-permute-done.1.first
  22.9 0.4 shard_map.79
  23.3 2.3 %collective-permute-start.3 = (s16[784,256]{1,0:T(8,128)(2,1)S(1)}, s16[784,256]{1,0:T(8,128)(2,1)S(1)}, u32[]{:S(2)}, u32[]{:S(2)}) collective-permute-start(s16[784,256]{1,0:T(8,128)(2,1)S(1)} %get-tuple-element.34), channel_id=1, source_target_pairs={{0,3},{1,2},{2,1},{3,0},{4,7},{5,6},{6,5},{7,4},{8,11},{9,10},{10,... | collective-permute-start | bytes 1204232 | tf_op jit(solution)/shard_map/ppermute | solution.py:394
  25.7 0.4 shard_map.82
  26.1 0.1 collective-permute-start.8
  26.2 1.2 %collective-permute-start.2 = (s16[784,256]{1,0:T(8,128)(2,1)S(1)}, s16[784,256]{1,0:T(8,128)(2,1)S(1)}, u32[]{:S(2)}, u32[]{:S(2)}) collective-permute-start(s16[784,256]{1,0:T(8,128)(2,1)S(1)} %get-tuple-element.33), channel_id=1, source_target_pairs={{0,3},{1,2},{2,1},{3,0},{4,7},{5,6},{6,5},{7,4},{8,11},{9,10},{10,... | collective-permute-start | bytes 1204232 | tf_op jit(solution)/shard_map/ppermute | solution.py:394
  27.4 5.9 %collective-permute-done.near = s16[1552,256]{1,0:T(8,128)(2,1)S(1)} collective-permute-done((s16[1552,256]{1,0:T(8,128)(2,1)}, s16[1552,256]{1,0:T(8,128)(2,1)S(1)}, u32[]{:S(2)}, u32[]{:S(2)}) %collective-permute-start) | collective-permute-done | bytes 794656 | tf_op jit(solution)/shard_map/ppermute | solution.py:394
  33.3 6.0 %collective-permute-done.3.far = s16[784,256]{1,0:T(8,128)(2,1)S(1)} collective-permute-done((s16[784,256]{1,0:T(8,128)(2,1)S(1)}, s16[784,256]{1,0:T(8,128)(2,1)S(1)}, u32[]{:S(2)}, u32[]{:S(2)}) %collective-permute-start.3) | collective-permute-done | bytes 401440 | tf_op jit(solution)/shard_map/ppermute | solution.py:394
  39.3 0.3 shard_map.80
  39.6 1.0 %collective-permute-start.4 = (s16[784,256]{1,0:T(8,128)(2,1)S(1)}, s16[784,256]{1,0:T(8,128)(2,1)S(1)}, u32[]{:S(2)}, u32[]{:S(2)}) collective-permute-start(s16[784,256]{1,0:T(8,128)(2,1)S(1)} %shard_map.80), channel_id=1, source_target_pairs={{0,4},{1,5},{2,6},{3,7},{4,0},{5,1},{6,2},{7,3},{8,12},{9,13},{10,... | collective-permute-start | bytes 1204232 | tf_op jit(solution)/shard_map/ppermute | solution.py:394
  40.6 0.1 collective-permute-start.7
  40.7 0.0 collective-permute-done.5.near
  40.7 0.0 collective-permute-done.8.far
  40.7 0.3 shard_map.83
  41.0 2.5 %collective-permute-start.9 = (s16[784,256]{1,0:T(8,128)(2,1)S(1)}, s16[784,256]{1,0:T(8,128)(2,1)S(1)}, u32[]{:S(2)}, u32[]{:S(2)}) collective-permute-start(s16[784,256]{1,0:T(8,128)(2,1)S(1)} %shard_map.83), channel_id=1, source_target_pairs={{0,12},{1,13},{2,14},{3,15},{4,8},{5,9},{6,10},{7,11},{8,4},{9,5},... | collective-permute-start | bytes 1204232 | tf_op jit(solution)/shard_map/ppermute | solution.py:394
  43.6 3.2 %collective-permute-done.4.third = s16[784,256]{1,0:T(8,128)(2,1)S(1)} collective-permute-done((s16[784,256]{1,0:T(8,128)(2,1)S(1)}, s16[784,256]{1,0:T(8,128)(2,1)S(1)}, u32[]{:S(2)}, u32[]{:S(2)}) %collective-permute-start.4) | collective-permute-done | bytes 401440 | tf_op jit(solution)/shard_map/ppermute | solution.py:394
  46.8 0.4 shard_map.81
  47.2 0.0 copy-start.5
  47.2 0.0 copy-start.6
  47.3 0.0 copy-start.4
  47.3 4.6 %collective-permute-start.10 = (s16[400,256]{1,0:T(8,128)(2,1)S(1)}, s16[400,256]{1,0:T(8,128)(2,1)S(1)}, u32[]{:S(2)}, u32[]{:S(2)}) collective-permute-start(s16[400,256]{1,0:T(8,128)(2,1)S(1)} %get-tuple-element.43), channel_id=1, source_target_pairs={{0,12},{1,13},{2,14},{3,15},{4,8},{5,9},{6,10},{7,11},{8,4},{9,5},... | collective-permute-start | bytes 614408 | tf_op jit(solution)/shard_map/ppermute | solution.py:394
  51.9 0.0 collective-permute-done.7.far
  51.9 0.0 collective-permute-done.9.third
  51.9 0.4 shard_map.84
  52.3 0.1 collective-permute-start.11
  52.4 2.6 %collective-permute-done.10.msg0 = s16[400,256]{1,0:T(8,128)(2,1)S(1)} collective-permute-done((s16[400,256]{1,0:T(8,128)(2,1)S(1)}, s16[400,256]{1,0:T(8,128)(2,1)S(1)}, u32[]{:S(2)}, u32[]{:S(2)}) %collective-permute-start.10) | collective-permute-done | bytes 204832 | tf_op jit(solution)/shard_map/ppermute | solution.py:394
  55.0 2.3 %collective-permute-done.11.msg1 = s16[400,256]{1,0:T(8,128)(2,1)S(1)} collective-permute-done((s16[400,256]{1,0:T(8,128)(2,1)S(1)}, s16[400,256]{1,0:T(8,128)(2,1)S(1)}, u32[]{:S(2)}, u32[]{:S(2)}) %collective-permute-start.11) | collective-permute-done | bytes 204832 | tf_op jit(solution)/shard_map/ppermute | solution.py:394
  57.3 0.2 shard_map.85
  57.5 7.2 %collective-permute-start.12 = (s16[208,512]{1,0:T(8,128)(2,1)S(1)}, s16[208,512]{1,0:T(8,128)(2,1)S(1)}, u32[]{:S(2)}, u32[]{:S(2)}) collective-permute-start(s16[208,512]{1,0:T(8,128)(2,1)S(1)} %get-tuple-element.46), channel_id=1, source_target_pairs={{0,16},{1,17},{2,18},{3,19},{4,20},{5,21},{6,22},{7,23},{8,24},{9,... | collective-permute-start | bytes 638984 | tf_op jit(solution)/shard_map/ppermute | solution.py:442
  64.8 0.4 shard_map.86
  65.2 2.9 %collective-permute-done.12.msg = s16[208,512]{1,0:T(8,128)(2,1)S(1)} collective-permute-done((s16[208,512]{1,0:T(8,128)(2,1)S(1)}, s16[208,512]{1,0:T(8,128)(2,1)S(1)}, u32[]{:S(2)}, u32[]{:S(2)}) %collective-permute-start.12) | collective-permute-done | bytes 213024 | tf_op jit(solution)/shard_map/ppermute | solution.py:442
  68.1 1.4 %shard_map.87 = (f32[192,512]{1,0:T(8,128)S(1)}, f32[24,512]{1,0:T(8,128)S(1)}) custom-call(f32[192,512]{1,0:T(8,128)S(1)} %get-tuple-element.45.mine, s16[208,512]{1,0:T(8,128)(2,1)S(1)} %collective-permute-done.12.msg, f32[192,512]{1,0:T(8,128)S(1)} %bitcast.7, f32[192,512]{1,0:T(8,128)S(1)} %get-tuple-element.47.wa, ...), custom_call_target="tpu_custom_call" | custom-call | flops 9437184 | bytes 2359296 | tf_op jit(solution)/shard_map/pallas_call | solution.py:154
  69.5 6.4 %collective-permute-start.13 = (f32[24,512]{1,0:T(8,128)S(1)}, f32[24,512]{1,0:T(8,128)S(1)}, u32[]{:S(2)}, u32[]{:S(2)}) collective-permute-start(f32[24,512]{1,0:T(8,128)S(1)} %get-tuple-element.50.kept), channel_id=1, source_target_pairs={{0,32},{32,0},{64,96},{96,64},{128,160},{160,128},{192,224},{224,1... | collective-permute-start | bytes 147464 | tf_op jit(solution)/shard_map/ppermute | solution.py:452
  76.0 0.9 %collective-permute-done.13 = f32[24,512]{1,0:T(8,128)S(1)} collective-permute-done((f32[24,512]{1,0:T(8,128)S(1)}, f32[24,512]{1,0:T(8,128)S(1)}, u32[]{:S(2)}, u32[]{:S(2)}) %collective-permute-start.13) | collective-permute-done | bytes 49184 | tf_op jit(solution)/shard_map/ppermute | solution.py:452
  76.8 0.1 collective-permute-start.14
  76.9 2.9 %collective-permute-done.14 = f32[24,512]{1,0:T(8,128)S(1)} collective-permute-done((f32[24,512]{1,0:T(8,128)S(1)}, f32[24,512]{1,0:T(8,128)S(1)}, u32[]{:S(2)}, u32[]{:S(2)}) %collective-permute-start.14) | collective-permute-done | bytes 49184 | tf_op jit(solution)/shard_map/ppermute | solution.py:452
  79.9 2.7 %collective-permute-start.15 = (f32[24,512]{1,0:T(8,128)S(1)}, f32[24,512]{1,0:T(8,128)S(1)}, u32[]{:S(2)}, u32[]{:S(2)}) collective-permute-start(f32[24,512]{1,0:T(8,128)S(1)} %add.24), channel_id=1, source_target_pairs={{0,128},{32,160},{64,192},{96,224},{128,0},{160,32},{192,64},{224,... | collective-permute-start | bytes 147464 | tf_op jit(solution)/shard_map/ppermute | solution.py:452
  82.6 2.2 %shard_map.89 = f32[192,512]{1,0:T(8,128)} custom-call(f32[192,512]{1,0:T(8,128)S(1)} %get-tuple-element.53.mom, f32[24,512]{1,0:T(8,128)S(1)} %get-tuple-element.50.kept, f32[192,512]{1,0:T(8,128)S(1)} %get-tuple-element.47.wa, bf16[1024,128]{1,0:T(8,128)(2,1)S(1)} %get-tuple-element.51.th, bf16[1024,128]{1,0:T(8,128)(2,1)S(1)} %get-tuple-element.52.tl), custom_call_target="tpu_custom_call" | custom-call | flops 7012352 | bytes 1753088 | tf_op jit(solution)/shard_map/pallas_call | solution.py:154
  84.8 0.0 collective-permute-done.15
  84.8 2.2 %shard_map.88 = f32[192,512]{1,0:T(8,128)} custom-call(f32[24,512]{1,0:T(8,128)S(1)} %add.25.total, f32[192,512]{1,0:T(8,128)S(1)} %get-tuple-element.47.wa, bf16[1024,128]{1,0:T(8,128)(2,1)S(1)} %get-tuple-element.51.th, bf16[1024,128]{1,0:T(8,128)(2,1)S(1)} %get-tuple-element.52.tl), custom_call_target="tpu_custom_call" | custom-call | flops 5439488 | bytes 1359872 | tf_op jit(solution)/shard_map/pallas_call | solution.py:154
  (16 shorter events, 0.1 us)
Async XLA Ops:
  10.0 12.8 %collective-permute-start.1 = (s16[1552,256]{1,0:T(8,128)(2,1)}, s16[1552,256]{1,0:T(8,128)(2,1)S(1)}, u32[]{:S(2)}, u32[]{:S(2)}) collective-permute-start(s16[1552,256]{1,0:T(8,128)(2,1)} %get-tuple-element.32), channel_id=1, source_target_pairs={{0,1},{1,0},{2,3},{3,2},{4,5},{5,4},{6,7},{7,6},{8,9},{9,8},{10,11... | collective-permute-start | bytes 2383880 | tf_op jit(solution)/shard_map/ppermute | solution.py:394
  12.2 13.4 %collective-permute-start.6 = (s16[1552,256]{1,0:T(8,128)(2,1)}, s16[1552,256]{1,0:T(8,128)(2,1)S(1)}, u32[]{:S(2)}, u32[]{:S(2)}) collective-permute-start(s16[1552,256]{1,0:T(8,128)(2,1)} %get-tuple-element.39), channel_id=1, source_target_pairs={{0,3},{1,2},{2,1},{3,0},{4,7},{5,6},{6,5},{7,4},{8,11},{9,10},{10,... | collective-permute-start | bytes 2383880 | tf_op jit(solution)/shard_map/ppermute | solution.py:394
  14.1 8.7 %copy-start.3 = (f32[8,192,256]{2,1,0:T(8,128)S(1)}, f32[8,192,256]{2,1,0:T(8,128)}, u32[]{:S(2)}) copy-start(f32[8,192,256]{2,1,0:T(8,128)} %get-tuple-element.31.own) | copy-start | bytes 4718596
  21.8 3.9 %copy-start.2 = (f32[8,192,256]{2,1,0:T(8,128)S(1)}, f32[8,192,256]{2,1,0:T(8,128)}, u32[]{:S(2)}) copy-start(f32[8,192,256]{2,1,0:T(8,128)} %get-tuple-element.38.own) | copy-start | bytes 4718596
  21.8 11.5 %collective-permute-start = (s16[1552,256]{1,0:T(8,128)(2,1)}, s16[1552,256]{1,0:T(8,128)(2,1)S(1)}, u32[]{:S(2)}, u32[]{:S(2)}) collective-permute-start(s16[1552,256]{1,0:T(8,128)(2,1)} %get-tuple-element.30), channel_id=1, source_target_pairs={{0,1},{1,0},{2,3},{3,2},{4,5},{5,4},{6,7},{7,6},{8,9},{9,8},{10,11... | collective-permute-start | bytes 2383880 | tf_op jit(solution)/shard_map/ppermute | solution.py:394
  22.3 18.4 %collective-permute-start.5 = (s16[1552,256]{1,0:T(8,128)(2,1)}, s16[1552,256]{1,0:T(8,128)(2,1)S(1)}, u32[]{:S(2)}, u32[]{:S(2)}) collective-permute-start(s16[1552,256]{1,0:T(8,128)(2,1)} %get-tuple-element.37), channel_id=1, source_target_pairs={{0,3},{1,2},{2,1},{3,0},{4,7},{5,6},{6,5},{7,4},{8,11},{9,10},{10,... | collective-permute-start | bytes 2383880 | tf_op jit(solution)/shard_map/ppermute | solution.py:394
  23.3 15.9 %copy-start.1 = (f32[8,192,256]{2,1,0:T(8,128)S(1)}, f32[8,192,256]{2,1,0:T(8,128)}, u32[]{:S(2)}) copy-start(f32[8,192,256]{2,1,0:T(8,128)} %get-tuple-element.29.own) | copy-start | bytes 4718596
  23.3 15.9 %collective-permute-start.3 = (s16[784,256]{1,0:T(8,128)(2,1)S(1)}, s16[784,256]{1,0:T(8,128)(2,1)S(1)}, u32[]{:S(2)}, u32[]{:S(2)}) collective-permute-start(s16[784,256]{1,0:T(8,128)(2,1)S(1)} %get-tuple-element.34), channel_id=1, source_target_pairs={{0,3},{1,2},{2,1},{3,0},{4,7},{5,6},{6,5},{7,4},{8,11},{9,10},{10,... | collective-permute-start | bytes 1204232 | tf_op jit(solution)/shard_map/ppermute | solution.py:394
  26.1 14.6 %collective-permute-start.8 = (s16[784,256]{1,0:T(8,128)(2,1)S(1)}, s16[784,256]{1,0:T(8,128)(2,1)S(1)}, u32[]{:S(2)}, u32[]{:S(2)}) collective-permute-start(s16[784,256]{1,0:T(8,128)(2,1)S(1)} %get-tuple-element.41), channel_id=1, source_target_pairs={{0,1},{1,0},{2,3},{3,2},{4,5},{5,4},{6,7},{7,6},{8,9},{9,8},{10,11... | collective-permute-start | bytes 1204232 | tf_op jit(solution)/shard_map/ppermute | solution.py:394
  26.2 17.4 %collective-permute-start.2 = (s16[784,256]{1,0:T(8,128)(2,1)S(1)}, s16[784,256]{1,0:T(8,128)(2,1)S(1)}, u32[]{:S(2)}, u32[]{:S(2)}) collective-permute-start(s16[784,256]{1,0:T(8,128)(2,1)S(1)} %get-tuple-element.33), channel_id=1, source_target_pairs={{0,3},{1,2},{2,1},{3,0},{4,7},{5,6},{6,5},{7,4},{8,11},{9,10},{10,... | collective-permute-start | bytes 1204232 | tf_op jit(solution)/shard_map/ppermute | solution.py:394
  39.3 1.4 %copy-start = (f32[8,192,256]{2,1,0:T(8,128)S(1)}, f32[8,192,256]{2,1,0:T(8,128)}, u32[]{:S(2)}) copy-start(f32[8,192,256]{2,1,0:T(8,128)} %get-tuple-element.36.own) | copy-start | bytes 4718596
  39.6 7.2 %collective-permute-start.4 = (s16[784,256]{1,0:T(8,128)(2,1)S(1)}, s16[784,256]{1,0:T(8,128)(2,1)S(1)}, u32[]{:S(2)}, u32[]{:S(2)}) collective-permute-start(s16[784,256]{1,0:T(8,128)(2,1)S(1)} %shard_map.80), channel_id=1, source_target_pairs={{0,4},{1,5},{2,6},{3,7},{4,0},{5,1},{6,2},{7,3},{8,12},{9,13},{10,... | collective-permute-start | bytes 1204232 | tf_op jit(solution)/shard_map/ppermute | solution.py:394
  40.6 11.3 %collective-permute-start.7 = (s16[784,256]{1,0:T(8,128)(2,1)S(1)}, s16[784,256]{1,0:T(8,128)(2,1)S(1)}, u32[]{:S(2)}, u32[]{:S(2)}) collective-permute-start(s16[784,256]{1,0:T(8,128)(2,1)S(1)} %get-tuple-element.40), channel_id=1, source_target_pairs={{0,1},{1,0},{2,3},{3,2},{4,5},{5,4},{6,7},{7,6},{8,9},{9,8},{10,11... | collective-permute-start | bytes 1204232 | tf_op jit(solution)/shard_map/ppermute | solution.py:394
  41.0 10.8 %collective-permute-start.9 = (s16[784,256]{1,0:T(8,128)(2,1)S(1)}, s16[784,256]{1,0:T(8,128)(2,1)S(1)}, u32[]{:S(2)}, u32[]{:S(2)}) collective-permute-start(s16[784,256]{1,0:T(8,128)(2,1)S(1)} %shard_map.83), channel_id=1, source_target_pairs={{0,12},{1,13},{2,14},{3,15},{4,8},{5,9},{6,10},{7,11},{8,4},{9,5},... | collective-permute-start | bytes 1204232 | tf_op jit(solution)/shard_map/ppermute | solution.py:394
  47.2 17.5 %copy-start.5 = (f32[64,64]{1,0:T(8,128)S(1)}, f32[64,64]{1,0:T(8,128)}, u32[]{:S(2)}) copy-start(f32[64,64]{1,0:T(8,128)} %constant.34.clone.table) | copy-start | bytes 49156
  47.2 17.5 %copy-start.6 = (s32[512]{0:T(512)S(1)}, s32[512]{0:T(512)}, u32[]{:S(2)}) copy-start(s32[512]{0:T(512)} %param.9) | copy-start | bytes 6148
  47.3 20.8 %copy-start.4 = (f32[1,192,512]{2,1,0:T(8,128)S(1)}, f32[1,192,512]{2,1,0:T(8,128)}, u32[]{:S(2)}) copy-start(f32[1,192,512]{2,1,0:T(8,128)} %param.8) | copy-start | bytes 1179652
  47.3 7.8 %collective-permute-start.10 = (s16[400,256]{1,0:T(8,128)(2,1)S(1)}, s16[400,256]{1,0:T(8,128)(2,1)S(1)}, u32[]{:S(2)}, u32[]{:S(2)}) collective-permute-start(s16[400,256]{1,0:T(8,128)(2,1)S(1)} %get-tuple-element.43), channel_id=1, source_target_pairs={{0,12},{1,13},{2,14},{3,15},{4,8},{5,9},{6,10},{7,11},{8,4},{9,5},... | collective-permute-start | bytes 614408 | tf_op jit(solution)/shard_map/ppermute | solution.py:394
  52.3 5.0 %collective-permute-start.11 = (s16[400,256]{1,0:T(8,128)(2,1)S(1)}, s16[400,256]{1,0:T(8,128)(2,1)S(1)}, u32[]{:S(2)}, u32[]{:S(2)}) collective-permute-start(s16[400,256]{1,0:T(8,128)(2,1)S(1)} %get-tuple-element.44), channel_id=1, source_target_pairs={{0,4},{1,5},{2,6},{3,7},{4,0},{5,1},{6,2},{7,3},{8,12},{9,13},{10,... | collective-permute-start | bytes 614408 | tf_op jit(solution)/shard_map/ppermute | solution.py:394
  57.5 10.6 %collective-permute-start.12 = (s16[208,512]{1,0:T(8,128)(2,1)S(1)}, s16[208,512]{1,0:T(8,128)(2,1)S(1)}, u32[]{:S(2)}, u32[]{:S(2)}) collective-permute-start(s16[208,512]{1,0:T(8,128)(2,1)S(1)} %get-tuple-element.46), channel_id=1, source_target_pairs={{0,16},{1,17},{2,18},{3,19},{4,20},{5,21},{6,22},{7,23},{8,24},{9,... | collective-permute-start | bytes 638984 | tf_op jit(solution)/shard_map/ppermute | solution.py:442
  69.5 7.3 %collective-permute-start.13 = (f32[24,512]{1,0:T(8,128)S(1)}, f32[24,512]{1,0:T(8,128)S(1)}, u32[]{:S(2)}, u32[]{:S(2)}) collective-permute-start(f32[24,512]{1,0:T(8,128)S(1)} %get-tuple-element.50.kept), channel_id=1, source_target_pairs={{0,32},{32,0},{64,96},{96,64},{128,160},{160,128},{192,224},{224,1... | collective-permute-start | bytes 147464 | tf_op jit(solution)/shard_map/ppermute | solution.py:452
  76.8 3.0 %collective-permute-start.14 = (f32[24,512]{1,0:T(8,128)S(1)}, f32[24,512]{1,0:T(8,128)S(1)}, u32[]{:S(2)}, u32[]{:S(2)}) collective-permute-start(f32[24,512]{1,0:T(8,128)S(1)} %add.23), channel_id=1, source_target_pairs={{0,64},{32,96},{64,0},{96,32},{128,192},{160,224},{192,128},{224,1... | collective-permute-start | bytes 147464 | tf_op jit(solution)/shard_map/ppermute | solution.py:452
  79.9 4.9 %collective-permute-start.15 = (f32[24,512]{1,0:T(8,128)S(1)}, f32[24,512]{1,0:T(8,128)S(1)}, u32[]{:S(2)}, u32[]{:S(2)}) collective-permute-start(f32[24,512]{1,0:T(8,128)S(1)} %add.24), channel_id=1, source_target_pairs={{0,128},{32,160},{64,192},{96,224},{128,0},{160,32},{192,64},{224,... | collective-permute-start | bytes 147464 | tf_op jit(solution)/shard_map/ppermute | solution.py:452

commit v2 on v1

--- a/solution.py
+++ b/solution.py
@@ -55,16 +55,42 @@
     return msg[HEAD + block * rows : HEAD + (block + 1) * rows, :].astype(jnp.int32).astype(F32) * scale
 
 
-def partial_kernel(outs, late, passed, tabs, acts, og, *rest):
+ORDERS = tuple((2, m1, m2, 0) for m1, m2 in CHAINS)
+
+
+def pair_of(late, place, i):
+    core, z, y, x = place // 32, (place // 16) % 2, (place // 4) % 4, place % 4
+    first = core == 0
+    u, v = jnp.where(first, x, y), jnp.where(first, y, x)
+    zr, a, b = i // 4, (i // 2) % 2, i % 2
+    far_half = (u // 2) ^ (1 - late)
+    yd = jnp.where(first, 2 * a + b, 2 * far_half + a)
+    xh = jnp.where(first, far_half, b)
+    halves = []
+    for s in range(2):
+        xd = 2 * xh + s
+        ud, vd = jnp.where(first, xd, yd), jnp.where(first, yd, xd)
+        j = vd ^ v
+        places = []
+        for order in ORDERS:
+            at = jnp.int32(0)
+            for k, value in enumerate(order):
+                at = jnp.where(j == value, k, at)
+            places.append(at * 2 + zr)
+        halves.append(((ud ^ u) % 2, places))
+    return (z ^ zr) * 8 + yd * 2 + xh, halves
+
+
+def partial_kernel(outs, late, passed, count, spot, acts, og, *rest):
     n = len(outs)
-    tab = tabs.at[late]
+    here = spot[0]
     rest = rest[passed:]
     out_refs = rest[:n]
     pieces, acc, peak, ready, in_sems, out_sems = rest[n + passed :]
-    count, rows, half = acc.shape[2:]
+    rows, half = acc.shape[3:]
 
     def fetch(i):
-        first = pl.multiple_of(tab[0, i] * 2 * rows, 128)
+        first = pl.multiple_of(pair_of(late, here, i)[0] * 2 * rows, 128)
         return pltpu.make_async_copy(acts.at[:, pl.ds(first, 2 * rows)], pieces.at[i], in_sems.at[i])
 
     for i in range(count):
@@ -74,15 +100,16 @@
     @pl.loop(0, count)
     def _(i):
         fetch(i).wait()
+        _, halves = pair_of(late, here, i)
         both = lax.dot_general(
             pieces[i], og[...], (((0,), (0,)), ((), ())), preferred_element_type=F32
         )
         for s in range(2):
-            slot = tab[1 + s, i]
+            slot, places = halves[s]
             part = both[s * rows : (s + 1) * rows]
             peak[slot] = jnp.maximum(peak[slot], column_peak(part))
             for c in range(2):
-                place = tab[3 + 2 * c + s, i]
+                place = places[c]
                 acc[c, slot, place] = part[:, c * half : (c + 1) * half]
                 for k, (k_slot, k_c, kind) in enumerate(outs):
                     if kind == "f" and k_c == c:
@@ -112,11 +139,11 @@
         copy.wait()
 
 
-def partials(outs, late, tab, acts, og, rows, through=()):
+def partials(outs, late, spot, acts, og, rows, through=()):
     tokens, _ = acts.shape
     width = og.shape[1]
     half = width // 2
-    count = tab.shape[2]
+    count = acts.shape[1] // rows // 4
     shapes = [
         jax.ShapeDtypeStruct((HEAD + count * rows, half), I16) if kind == "q" else f32(count, rows, half)
         for _, _, kind in outs
@@ -124,7 +151,7 @@
     messages = sum(kind == "q" for _, _, kind in outs)
     anywhere = pl.BlockSpec(memory_space=pl.ANY)
     return pl.pallas_call(
-        functools.partial(partial_kernel, outs, late, len(through)),
+        functools.partial(partial_kernel, outs, late, len(through), count),
         in_specs=[pl.BlockSpec(memory_space=pltpu.SMEM), anywhere, pl.BlockSpec(memory_space=pltpu.VMEM)]
         + [anywhere] * len(through),
         out_specs=[anywhere] * (len(outs) + len(through)),
@@ -142,7 +169,7 @@
         cost_estimate=pl.CostEstimate(
             flops=2 * tokens * count * 2 * rows * width, bytes_accessed=tokens * count * 2 * rows * 2, transcendentals=0
         ),
-    )(tab, acts, og, *through)
+    )(spot, acts, og, *through)
 
 
 def whole(shape, index=None):
@@ -171,21 +198,21 @@
     return jax.ShapeDtypeStruct(shape, F32)
 
 
-def second_kernel(own, first, out_a, out_b, held):
+def second_kernel(start, own, first, *rest):
+    out, held = rest[-2:]
     rows = own.shape[1]
-    quarter = own.shape[0] // 2
+    count = own.shape[0]
     scale = scale_of(first)
-    for out, start in ((out_a, 0), (out_b, quarter)):
-        peak = None
-        for b in range(quarter):
-            x = own[start + b] + dequantise(first, start + b, rows, scale)
-            held[b] = x
-            p = column_peak(x)
-            peak = p if peak is None else jnp.maximum(peak, p)
-        code = scale_code(peak)
-        put_head(out, code)
-        for b in range(quarter):
-            out[HEAD + b * rows : HEAD + (b + 1) * rows, :] = quantise(held[b], code)
+    peak = None
+    for b in range(count):
+        x = own[b] + dequantise(first, start + b, rows, scale)
+        held[b] = x
+        p = column_peak(x)
+        peak = p if peak is None else jnp.maximum(peak, p)
+    code = scale_code(peak)
+    put_head(out, code)
+    for b in range(count):
+        out[HEAD + b * rows : HEAD + (b + 1) * rows, :] = quantise(held[b], code)
 
 
 def third_kernel(own, near, far, out, held):
@@ -347,37 +374,13 @@
     return [(rep * 32 + f, rep * 32 + (f ^ 16)) for rep in range(8) for f in range(32)]
 
 
-ORDERS = tuple((2, m1, m2, 0) for m1, m2 in CHAINS)
-
-
-def tables():
-    found = np.zeros((2, 32, 2, 7, 8), np.int32)
-    for core in range(2):
-        for f in range(32):
-            z, y, x = coords(f)
-            u, v = (x, y) if core == 0 else (y, x)
-            for late in range(2):
-                far_half = (u >> 1) ^ (1 - late)
-                for i in range(8):
-                    zr, a, b = i // 4, (i // 2) % 2, i % 2
-                    yd, xh = (2 * a + b, far_half) if core == 0 else (2 * far_half + a, b)
-                    column = [(z ^ zr) * 8 + yd * 2 + xh]
-                    both = [((2 * xh + s, yd) if core == 0 else (yd, 2 * xh + s)) for s in range(2)]
-                    column += [(ud ^ u) & 1 for ud, _ in both]
-                    for order in ORDERS:
-                        column += [order.index(vd ^ v) * 2 + zr for _, vd in both]
-                    found[core, f, late, :, i] = column
-    return found.reshape(64, 2, 7, 8)
-
-
 def shards(activations, out_grads, momentum, band):
     acts, og, momentum = activations[0], out_grads[0], momentum[0]
     rows, width = momentum.shape
     half = width // 2
     axes = ("rep", "fsdp")
     core = lax.axis_index("rep") % 2
-    place = core * 32 + lax.axis_index("fsdp")
-    tab = lax.dynamic_index_in_dim(jnp.asarray(tables()), place, keepdims=False)
+    spot = (core * 32 + lax.axis_index("fsdp")).reshape(1)
 
     table = jnp.asarray(dct_table(GROUP).T)
     n = band.shape[0]
@@ -393,10 +396,10 @@
     def swap(x, step, late):
         return lax.ppermute(x, axes, partner_pairs(step, late))
 
-    m1a0, m1a1, m1b1, own0 = partials(((0, 0, "q"), (0, 1, "q"), (1, 1, "q"), (1, 0, "f")), 0, tab, acts, og, rows)
+    m1a0, m1a1, m1b1, own0 = partials(((0, 0, "q"), (0, 1, "q"), (1, 1, "q"), (1, 0, "f")), 0, spot, acts, og, rows)
     r1a = [swap(m1a0, CHAINS[0][0], False), swap(m1a1, CHAINS[1][0], False)]
     m1b0, own1, keep0, keep1, m1b1 = partials(
-        ((1, 0, "q"), (1, 1, "f"), (0, 0, "f"), (0, 1, "f")), 1, tab, acts, og, rows, (m1b1,)
+        ((1, 0, "q"), (1, 1, "f"), (0, 0, "f"), (0, 1, "f")), 1, spot, acts, og, rows, (m1b1,)
     )
     r1b = [swap(m1b0, CHAINS[0][0], False), swap(m1b1, CHAINS[1][0], False)]
     own, keep = [own0, own1], [keep0, keep1]
@@ -404,20 +407,24 @@
     msg8, msg4, msg2 = i16(8 * rows, half), i16(4 * rows, half), i16(2 * rows, half)
     four = (4, rows, half)
     kept4, r4 = [], []
-    r2, r3 = [], []
-    for c, (m1, m2) in enumerate(CHAINS):
-        m2a, m2b = call(
-            second_kernel,
-            (own[c], r1a[c]),
-            [whole((8, rows, half)), whole(msg8.shape)],
-            [msg4, msg4],
+    r3 = []
+
+    def second(c, part, after=()):
+        (m,) = call(
+            functools.partial(second_kernel, 4 * part),
+            (own[c], r1a[c], *after),
+            [whole(four, (part, 0, 0)), whole(msg8.shape)] + [pl.BlockSpec(memory_space=pl.ANY)] * len(after),
+            [msg4],
             [pltpu.VMEM(four, F32)],
         )
-        r2.append((swap(m2a, m2, False), swap(m2b, m2, False)))
+        return swap(m, CHAINS[c][1], False)
+
+    r2a = [second(c, 0) for c in range(2)]
+    r2b = [second(c, 1, (r1b[1 - c],)) for c in range(2)]
     for c, (m1, m2) in enumerate(CHAINS):
         (m3,) = call(
             third_kernel,
-            (keep[c], r1b[c], r2[c][0]),
+            (keep[c], r1b[c], r2a[c]),
             [whole(four), whole(msg4.shape), whole(msg4.shape)],
             [msg4],
             [pltpu.VMEM(four, F32)],
@@ -426,7 +433,7 @@
     for c, (m1, m2) in enumerate(CHAINS):
         m4, k4 = call(
             fourth_kernel,
-            (keep[c], r1b[c], r2[c][1], r3[c]),
+            (keep[c], r1b[c], r2b[c], r3[c]),
             [whole(four, (1, 0, 0)), whole(msg8.shape), whole(msg4.shape), whole(msg4.shape)],
             [msg2, f32(2, rows, half)],
             [pltpu.VMEM((2, rows, half), F32)],

time: 87.2 us -> 85.1 us (0.976)
  waiting for transfers between devices: 26.7 us -> 22.8 us
  starting transfers between devices: 33.7 us -> 36 us
  local copies, waits for them, and re-layouts: 1.34 us -> 0.09 us
    ppermute x12, waiting for transfers between devices: 20 us -> 17.6 us  [swap(): return lax.ppermute(x, axes, partner_pairs(step, late))]
    ppermute x3, starting transfers between devices: 9.25 us -> 10.9 us  [shards(): lax.ppermute(total, 'rep', [(r, r ^ bit) for r in range(REPS)])]
    ppermute x3, waiting for transfers between devices: 3.81 us -> 2.36 us  [shards(): lax.ppermute(total, 'rep', [(r, r ^ bit) for r in range(REPS)])]
    squeeze x2 -> x0, local copies, waits for them, and re-layouts: 1.3 us -> none  [shards(): tab = lax.dynamic_index_in_dim(jnp.asarray(tables()), place, keepdims=False)]
    ppermute x12, starting transfers between devices: 17.2 us -> 18.2 us  [swap(): return lax.ppermute(x, axes, partner_pairs(step, late))]
    pallas_call x11 -> x13, Pallas kernels: 8.78 us -> 8.8 us  [call(): pl.pallas_call(kernel, grid=(1,), in_specs=in_specs, out_specs=[whole(o.s...]
  transfers between devices with their start and end apart: 16 -> 16, of which waited for: 8 -> 8; matrix products, arithmetic and copies ran while one was open for 0% -> 0% of each run, Pallas kernels for 14% -> 15%
where the time goes in v2:
time: 85.1 us; the launch traced here: 84.4 us
  starting transfers between devices  36 us (42%)
  Pallas kernels  24.6 us (29%)
  waiting for transfers between devices  22.8 us (27%)
    ppermute x12, starting transfers between devices, swap(): return lax.ppermute(x, axes, partner_pairs(step, late))  18.2 us
    ppermute x12, waiting for transfers between devices, swap(): return lax.ppermute(x, axes, partner_pairs(step, late))  17.6 us
    pallas_call x2, Pallas kernels, partials(): pl.pallas_call(functools.partial(partial_kernel, outs, late, len(through)...  15.8 us
    ppermute x3, starting transfers between devices, shards(): lax.ppermute(total, 'rep', [(r, r ^ bit) for r in range(REPS)])  10.9 us
    pallas_call x13, Pallas kernels, call(): pl.pallas_call(kernel, grid=(1,), in_specs=in_specs, out_specs=[whole(o.s...  8.8 us
    ppermute x1, starting transfers between devices, shards(): r5 = lax.ppermute(m5, axes, far_pairs())  6.99 us
    ppermute x1, waiting for transfers between devices, shards(): r5 = lax.ppermute(m5, axes, far_pairs())  2.88 us
    ppermute x3, waiting for transfers between devices, shards(): lax.ppermute(total, 'rep', [(r, r ^ bit) for r in range(REPS)])  2.36 us
  transfers between devices with their start and end apart: 16, of which 8 were waited for; matrix products, arithmetic and copies ran while one was open for 0% of the time, Pallas kernels for 15%

profile of v2, /device:TPU:1, one launch (start us, length us, event | category | flops | bytes accessed | tf_op | source)
XLA Modules:
  0.0 84.4 jit_solution(2542127890622802755)
XLA Ops:
  0.6 8.1 %shard_map.68 = (s16[1552,256]{1,0:T(8,128)(2,1)}, s16[1552,256]{1,0:T(8,128)(2,1)}, s16[1552,256]{1,0:T(8,128)(2,1)}, f32[8,192,256]{2,1,0:T(8,128)}) custom-call(s32[1]{0:T(128)} %bitcast.spot, bf16[768,6144]{1,0:T(8,128)(2,1)} %bitcast.8, bf16[768,512]{1,0:T(8,128)(2,1)} %bitcast.10), custom_call_target="tpu_custom_call" | custom-call | flops 2415919104 | bytes 4718592 | tf_op jit(solution)/shard_map/pallas_call | solution.py:153
  8.8 2.2 %collective-permute-start.1 = (s16[1552,256]{1,0:T(8,128)(2,1)}, s16[1552,256]{1,0:T(8,128)(2,1)S(1)}, u32[]{:S(2)}, u32[]{:S(2)}) collective-permute-start(s16[1552,256]{1,0:T(8,128)(2,1)} %get-tuple-element.28), channel_id=1, source_target_pairs={{0,1},{1,0},{2,3},{3,2},{4,5},{5,4},{6,7},{7,6},{8,9},{9,8},{10,11... | collective-permute-start | bytes 2383880 | tf_op jit(solution)/shard_map/ppermute | solution.py:397
  11.0 1.9 %collective-permute-start.6 = (s16[1552,256]{1,0:T(8,128)(2,1)}, s16[1552,256]{1,0:T(8,128)(2,1)S(1)}, u32[]{:S(2)}, u32[]{:S(2)}) collective-permute-start(s16[1552,256]{1,0:T(8,128)(2,1)} %get-tuple-element.33), channel_id=1, source_target_pairs={{0,3},{1,2},{2,1},{3,0},{4,7},{5,6},{6,5},{7,4},{8,11},{9,10},{10,... | collective-permute-start | bytes 2383880 | tf_op jit(solution)/shard_map/ppermute | solution.py:397
  12.9 7.7 %shard_map.69 = (s16[1552,256]{1,0:T(8,128)(2,1)}, f32[8,192,256]{2,1,0:T(8,128)}, f32[8,192,256]{2,1,0:T(8,128)}, f32[8,192,256]{2,1,0:T(8,128)}, s16[1552,256]{1,0:T(8,128)(2,1)}) custom-call(s32[1]{0:T(128)} %bitcast.spot, bf16[768,6144]{1,0:T(8,128)(2,1)} %bitcast.9, bf16[768,512]{1,0:T(8,128)(2,1)} %bitcast.11, ...), custom_call_target="tpu_custom_call", output_to_operand_aliasing={{4}: (3, {})} | custom-call | flops 2415919104 | bytes 4718592 | tf_op jit(solution)/shard_map/pallas_call | solution.py:153
  20.6 0.9 %collective-permute-start.2 = (s16[1552,256]{1,0:T(8,128)(2,1)}, s16[1552,256]{1,0:T(8,128)(2,1)S(1)}, u32[]{:S(2)}, u32[]{:S(2)}) collective-permute-start(s16[1552,256]{1,0:T(8,128)(2,1)} %get-tuple-element.29), channel_id=1, source_target_pairs={{0,3},{1,2},{2,1},{3,0},{4,7},{5,6},{6,5},{7,4},{8,11},{9,10},{10,... | collective-permute-start | bytes 2383880 | tf_op jit(solution)/shard_map/ppermute | solution.py:397
  21.5 0.0 collective-permute-start
  21.5 0.0 collective-permute-done.1.first
  21.5 0.2 shard_map.71
  21.7 2.5 %collective-permute-start.4 = (s16[784,256]{1,0:T(8,128)(2,1)S(1)}, s16[784,256]{1,0:T(8,128)(2,1)S(1)}, u32[]{:S(2)}, u32[]{:S(2)}) collective-permute-start(s16[784,256]{1,0:T(8,128)(2,1)S(1)} %shard_map.71), channel_id=1, source_target_pairs={{0,3},{1,2},{2,1},{3,0},{4,7},{5,6},{6,5},{7,4},{8,11},{9,10},{10,... | collective-permute-start | bytes 1204232 | tf_op jit(solution)/shard_map/ppermute | solution.py:397
  24.2 0.0 collective-permute-done.6.first
  24.2 0.2 shard_map.75
  24.4 0.4 collective-permute-start.8
  24.9 8.4 %collective-permute-done.2.rest_0_.near = s16[1552,256]{1,0:T(8,128)(2,1)S(1)} collective-permute-done((s16[1552,256]{1,0:T(8,128)(2,1)}, s16[1552,256]{1,0:T(8,128)(2,1)S(1)}, u32[]{:S(2)}, u32[]{:S(2)}) %collective-permute-start.2) | collective-permute-done | bytes 794656 | tf_op jit(solution)/shard_map/ppermute | solution.py:397
  33.3 0.2 shard_map.70
  33.5 0.9 %collective-permute-start.3 = (s16[784,256]{1,0:T(8,128)(2,1)S(1)}, s16[784,256]{1,0:T(8,128)(2,1)S(1)}, u32[]{:S(2)}, u32[]{:S(2)}) collective-permute-start(s16[784,256]{1,0:T(8,128)(2,1)S(1)} %shard_map.70), channel_id=1, source_target_pairs={{0,3},{1,2},{2,1},{3,0},{4,7},{5,6},{6,5},{7,4},{8,11},{9,10},{10,... | collective-permute-start | bytes 1204232 | tf_op jit(solution)/shard_map/ppermute | solution.py:397
  34.4 0.0 collective-permute-done.near.rest_0_
  34.4 3.2 %collective-permute-done.4.far = s16[784,256]{1,0:T(8,128)(2,1)S(1)} collective-permute-done((s16[784,256]{1,0:T(8,128)(2,1)S(1)}, s16[784,256]{1,0:T(8,128)(2,1)S(1)}, u32[]{:S(2)}, u32[]{:S(2)}) %collective-permute-start.4) | collective-permute-done | bytes 401440 | tf_op jit(solution)/shard_map/ppermute | solution.py:397
  37.6 0.3 shard_map.72
  37.9 1.0 %collective-permute-start.5 = (s16[784,256]{1,0:T(8,128)(2,1)S(1)}, s16[784,256]{1,0:T(8,128)(2,1)S(1)}, u32[]{:S(2)}, u32[]{:S(2)}) collective-permute-start(s16[784,256]{1,0:T(8,128)(2,1)S(1)} %shard_map.72), channel_id=1, source_target_pairs={{0,4},{1,5},{2,6},{3,7},{4,0},{5,1},{6,2},{7,3},{8,12},{9,13},{10,... | collective-permute-start | bytes 1204232 | tf_op jit(solution)/shard_map/ppermute | solution.py:397
  39.0 0.2 shard_map.74
  39.2 0.1 collective-permute-start.7
  39.3 0.0 collective-permute-done.8.far
  39.3 0.1 copy-done
  39.3 0.3 shard_map.76
  39.7 2.6 %collective-permute-start.9 = (s16[784,256]{1,0:T(8,128)(2,1)S(1)}, s16[784,256]{1,0:T(8,128)(2,1)S(1)}, u32[]{:S(2)}, u32[]{:S(2)}) collective-permute-start(s16[784,256]{1,0:T(8,128)(2,1)S(1)} %shard_map.76), channel_id=1, source_target_pairs={{0,12},{1,13},{2,14},{3,15},{4,8},{5,9},{6,10},{7,11},{8,4},{9,5},... | collective-permute-start | bytes 1204232 | tf_op jit(solution)/shard_map/ppermute | solution.py:397
  42.2 0.0 collective-permute-done.3.far
  42.2 2.8 %collective-permute-done.5.third = s16[784,256]{1,0:T(8,128)(2,1)S(1)} collective-permute-done((s16[784,256]{1,0:T(8,128)(2,1)S(1)}, s16[784,256]{1,0:T(8,128)(2,1)S(1)}, u32[]{:S(2)}, u32[]{:S(2)}) %collective-permute-start.5) | collective-permute-done | bytes 401440 | tf_op jit(solution)/shard_map/ppermute | solution.py:397
  45.0 0.4 shard_map.73
  45.5 0.0 copy-start.5
  45.5 0.0 copy-start.6
  45.5 0.0 copy-start.4
  45.5 4.1 %collective-permute-start.10 = (s16[400,256]{1,0:T(8,128)(2,1)S(1)}, s16[400,256]{1,0:T(8,128)(2,1)S(1)}, u32[]{:S(2)}, u32[]{:S(2)}) collective-permute-start(s16[400,256]{1,0:T(8,128)(2,1)S(1)} %get-tuple-element.35), channel_id=1, source_target_pairs={{0,12},{1,13},{2,14},{3,15},{4,8},{5,9},{6,10},{7,11},{8,4},{9,5},... | collective-permute-start | bytes 614408 | tf_op jit(solution)/shard_map/ppermute | solution.py:397
  49.6 0.4 shard_map.77
  50.1 1.6 %collective-permute-start.11 = (s16[400,256]{1,0:T(8,128)(2,1)S(1)}, s16[400,256]{1,0:T(8,128)(2,1)S(1)}, u32[]{:S(2)}, u32[]{:S(2)}) collective-permute-start(s16[400,256]{1,0:T(8,128)(2,1)S(1)} %get-tuple-element.36), channel_id=1, source_target_pairs={{0,4},{1,5},{2,6},{3,7},{4,0},{5,1},{6,2},{7,3},{8,12},{9,13},{10,... | collective-permute-start | bytes 614408 | tf_op jit(solution)/shard_map/ppermute | solution.py:397
  51.6 1.1 %collective-permute-done.10.msg0 = s16[400,256]{1,0:T(8,128)(2,1)S(1)} collective-permute-done((s16[400,256]{1,0:T(8,128)(2,1)S(1)}, s16[400,256]{1,0:T(8,128)(2,1)S(1)}, u32[]{:S(2)}, u32[]{:S(2)}) %collective-permute-start.10) | collective-permute-done | bytes 204832 | tf_op jit(solution)/shard_map/ppermute | solution.py:397
  52.8 2.0 %collective-permute-done.11.msg1 = s16[400,256]{1,0:T(8,128)(2,1)S(1)} collective-permute-done((s16[400,256]{1,0:T(8,128)(2,1)S(1)}, s16[400,256]{1,0:T(8,128)(2,1)S(1)}, u32[]{:S(2)}, u32[]{:S(2)}) %collective-permute-start.11) | collective-permute-done | bytes 204832 | tf_op jit(solution)/shard_map/ppermute | solution.py:397
  54.8 0.2 shard_map.78
  55.0 7.0 %collective-permute-start.12 = (s16[208,512]{1,0:T(8,128)(2,1)S(1)}, s16[208,512]{1,0:T(8,128)(2,1)S(1)}, u32[]{:S(2)}, u32[]{:S(2)}) collective-permute-start(s16[208,512]{1,0:T(8,128)(2,1)S(1)} %get-tuple-element.38), channel_id=1, source_target_pairs={{0,16},{1,17},{2,18},{3,19},{4,20},{5,21},{6,22},{7,23},{8,24},{9,... | collective-permute-start | bytes 638984 | tf_op jit(solution)/shard_map/ppermute | solution.py:449
  62.0 0.4 shard_map.79
  62.4 2.9 %collective-permute-done.12.msg = s16[208,512]{1,0:T(8,128)(2,1)S(1)} collective-permute-done((s16[208,512]{1,0:T(8,128)(2,1)S(1)}, s16[208,512]{1,0:T(8,128)(2,1)S(1)}, u32[]{:S(2)}, u32[]{:S(2)}) %collective-permute-start.12) | collective-permute-done | bytes 213024 | tf_op jit(solution)/shard_map/ppermute | solution.py:449
  65.3 1.4 %shard_map.80 = (f32[192,512]{1,0:T(8,128)S(1)}, f32[24,512]{1,0:T(8,128)S(1)}) custom-call(f32[192,512]{1,0:T(8,128)S(1)} %get-tuple-element.37.mine, s16[208,512]{1,0:T(8,128)(2,1)S(1)} %collective-permute-done.12.msg, f32[192,512]{1,0:T(8,128)S(1)} %bitcast.6, f32[192,512]{1,0:T(8,128)S(1)} %get-tuple-element.39.wa, ...), custom_call_target="tpu_custom_call" | custom-call | flops 9437184 | bytes 2359296 | tf_op jit(solution)/shard_map/pallas_call | solution.py:181
  66.7 6.0 %collective-permute-start.13 = (f32[24,512]{1,0:T(8,128)S(1)}, f32[24,512]{1,0:T(8,128)S(1)}, u32[]{:S(2)}, u32[]{:S(2)}) collective-permute-start(f32[24,512]{1,0:T(8,128)S(1)} %get-tuple-element.42.kept), channel_id=1, source_target_pairs={{0,32},{32,0},{64,96},{96,64},{128,160},{160,128},{192,224},{224,1... | collective-permute-start | bytes 147464 | tf_op jit(solution)/shard_map/ppermute | solution.py:459
  72.7 0.9 %collective-permute-done.13 = f32[24,512]{1,0:T(8,128)S(1)} collective-permute-done((f32[24,512]{1,0:T(8,128)S(1)}, f32[24,512]{1,0:T(8,128)S(1)}, u32[]{:S(2)}, u32[]{:S(2)}) %collective-permute-start.13) | collective-permute-done | bytes 49184 | tf_op jit(solution)/shard_map/ppermute | solution.py:459
  73.6 1.9 %collective-permute-start.14 = (f32[24,512]{1,0:T(8,128)S(1)}, f32[24,512]{1,0:T(8,128)S(1)}, u32[]{:S(2)}, u32[]{:S(2)}) collective-permute-start(f32[24,512]{1,0:T(8,128)S(1)} %add.18), channel_id=1, source_target_pairs={{0,64},{32,96},{64,0},{96,32},{128,192},{160,224},{192,128},{224,1... | collective-permute-start | bytes 147464 | tf_op jit(solution)/shard_map/ppermute | solution.py:459
  75.5 1.5 %collective-permute-done.14 = f32[24,512]{1,0:T(8,128)S(1)} collective-permute-done((f32[24,512]{1,0:T(8,128)S(1)}, f32[24,512]{1,0:T(8,128)S(1)}, u32[]{:S(2)}, u32[]{:S(2)}) %collective-permute-start.14) | collective-permute-done | bytes 49184 | tf_op jit(solution)/shard_map/ppermute | solution.py:459
  77.0 3.0 %collective-permute-start.15 = (f32[24,512]{1,0:T(8,128)S(1)}, f32[24,512]{1,0:T(8,128)S(1)}, u32[]{:S(2)}, u32[]{:S(2)}) collective-permute-start(f32[24,512]{1,0:T(8,128)S(1)} %add.19), channel_id=1, source_target_pairs={{0,128},{32,160},{64,192},{96,224},{128,0},{160,32},{192,64},{224,... | collective-permute-start | bytes 147464 | tf_op jit(solution)/shard_map/ppermute | solution.py:459
  80.0 2.2 %shard_map.82 = f32[192,512]{1,0:T(8,128)} custom-call(f32[192,512]{1,0:T(8,128)S(1)} %get-tuple-element.45.mom, f32[24,512]{1,0:T(8,128)S(1)} %get-tuple-element.42.kept, f32[192,512]{1,0:T(8,128)S(1)} %get-tuple-element.39.wa, bf16[1024,128]{1,0:T(8,128)(2,1)S(1)} %get-tuple-element.43.th, bf16[1024,128]{1,0:T(8,128)(2,1)S(1)} %get-tuple-element.44.tl), custom_call_target="tpu_custom_call" | custom-call | flops 7012352 | bytes 1753088 | tf_op jit(solution)/shard_map/pallas_call | solution.py:181
  82.2 2.2 %shard_map.81 = f32[192,512]{1,0:T(8,128)} custom-call(f32[24,512]{1,0:T(8,128)S(1)} %add.20.total, f32[192,512]{1,0:T(8,128)S(1)} %get-tuple-element.39.wa, bf16[1024,128]{1,0:T(8,128)(2,1)S(1)} %get-tuple-element.43.th, bf16[1024,128]{1,0:T(8,128)(2,1)S(1)} %get-tuple-element.44.tl), custom_call_target="tpu_custom_call" | custom-call | flops 5439488 | bytes 1359872 | tf_op jit(solution)/shard_map/pallas_call | solution.py:181
  (16 shorter events, 0.1 us)
Async XLA Ops:
  8.8 12.7 %collective-permute-start.1 = (s16[1552,256]{1,0:T(8,128)(2,1)}, s16[1552,256]{1,0:T(8,128)(2,1)S(1)}, u32[]{:S(2)}, u32[]{:S(2)}) collective-permute-start(s16[1552,256]{1,0:T(8,128)(2,1)} %get-tuple-element.28), channel_id=1, source_target_pairs={{0,1},{1,0},{2,3},{3,2},{4,5},{5,4},{6,7},{7,6},{8,9},{9,8},{10,11... | collective-permute-start | bytes 2383880 | tf_op jit(solution)/shard_map/ppermute | solution.py:397
  11.0 13.2 %collective-permute-start.6 = (s16[1552,256]{1,0:T(8,128)(2,1)}, s16[1552,256]{1,0:T(8,128)(2,1)S(1)}, u32[]{:S(2)}, u32[]{:S(2)}) collective-permute-start(s16[1552,256]{1,0:T(8,128)(2,1)} %get-tuple-element.33), channel_id=1, source_target_pairs={{0,3},{1,2},{2,1},{3,0},{4,7},{5,6},{6,5},{7,4},{8,11},{9,10},{10,... | collective-permute-start | bytes 2383880 | tf_op jit(solution)/shard_map/ppermute | solution.py:397
  12.9 8.6 %copy-start.3 = (f32[8,192,256]{2,1,0:T(8,128)S(1)}, f32[8,192,256]{2,1,0:T(8,128)}, u32[]{:S(2)}) copy-start(f32[8,192,256]{2,1,0:T(8,128)} %get-tuple-element.27.own) | copy-start | bytes 4718596
  20.6 3.6 %copy-start.2 = (f32[8,192,256]{2,1,0:T(8,128)S(1)}, f32[8,192,256]{2,1,0:T(8,128)}, u32[]{:S(2)}) copy-start(f32[8,192,256]{2,1,0:T(8,128)} %get-tuple-element.32.own) | copy-start | bytes 4718596
  20.6 12.7 %collective-permute-start.2 = (s16[1552,256]{1,0:T(8,128)(2,1)}, s16[1552,256]{1,0:T(8,128)(2,1)S(1)}, u32[]{:S(2)}, u32[]{:S(2)}) collective-permute-start(s16[1552,256]{1,0:T(8,128)(2,1)} %get-tuple-element.29), channel_id=1, source_target_pairs={{0,3},{1,2},{2,1},{3,0},{4,7},{5,6},{6,5},{7,4},{8,11},{9,10},{10,... | collective-permute-start | bytes 2383880 | tf_op jit(solution)/shard_map/ppermute | solution.py:397
  21.5 13.0 %collective-permute-start = (s16[1552,256]{1,0:T(8,128)(2,1)}, s16[1552,256]{1,0:T(8,128)(2,1)S(1)}, u32[]{:S(2)}, u32[]{:S(2)}) collective-permute-start(s16[1552,256]{1,0:T(8,128)(2,1)} %get-tuple-element.26), channel_id=1, source_target_pairs={{0,1},{1,0},{2,3},{3,2},{4,5},{5,4},{6,7},{7,6},{8,9},{9,8},{10,11... | collective-permute-start | bytes 2383880 | tf_op jit(solution)/shard_map/ppermute | solution.py:397
  21.7 15.9 %collective-permute-start.4 = (s16[784,256]{1,0:T(8,128)(2,1)S(1)}, s16[784,256]{1,0:T(8,128)(2,1)S(1)}, u32[]{:S(2)}, u32[]{:S(2)}) collective-permute-start(s16[784,256]{1,0:T(8,128)(2,1)S(1)} %shard_map.71), channel_id=1, source_target_pairs={{0,3},{1,2},{2,1},{3,0},{4,7},{5,6},{6,5},{7,4},{8,11},{9,10},{10,... | collective-permute-start | bytes 1204232 | tf_op jit(solution)/shard_map/ppermute | solution.py:397
  24.4 13.2 %copy-start.1 = (f32[8,192,256]{2,1,0:T(8,128)S(1)}, f32[8,192,256]{2,1,0:T(8,128)}, u32[]{:S(2)}) copy-start(f32[8,192,256]{2,1,0:T(8,128)} %get-tuple-element.25.own) | copy-start | bytes 4718596
  24.4 14.9 %collective-permute-start.8 = (s16[784,256]{1,0:T(8,128)(2,1)S(1)}, s16[784,256]{1,0:T(8,128)(2,1)S(1)}, u32[]{:S(2)}, u32[]{:S(2)}) collective-permute-start(s16[784,256]{1,0:T(8,128)(2,1)S(1)} %shard_map.75), channel_id=1, source_target_pairs={{0,1},{1,0},{2,3},{3,2},{4,5},{5,4},{6,7},{7,6},{8,9},{9,8},{10,11... | collective-permute-start | bytes 1204232 | tf_op jit(solution)/shard_map/ppermute | solution.py:397
  33.5 8.7 %collective-permute-start.3 = (s16[784,256]{1,0:T(8,128)(2,1)S(1)}, s16[784,256]{1,0:T(8,128)(2,1)S(1)}, u32[]{:S(2)}, u32[]{:S(2)}) collective-permute-start(s16[784,256]{1,0:T(8,128)(2,1)S(1)} %shard_map.70), channel_id=1, source_target_pairs={{0,3},{1,2},{2,1},{3,0},{4,7},{5,6},{6,5},{7,4},{8,11},{9,10},{10,... | collective-permute-start | bytes 1204232 | tf_op jit(solution)/shard_map/ppermute | solution.py:397
  37.9 1.4 %copy-start = (f32[8,192,256]{2,1,0:T(8,128)S(1)}, f32[8,192,256]{2,1,0:T(8,128)}, u32[]{:S(2)}) copy-start(f32[8,192,256]{2,1,0:T(8,128)} %get-tuple-element.31.own) | copy-start | bytes 4718596
  37.9 7.1 %collective-permute-start.5 = (s16[784,256]{1,0:T(8,128)(2,1)S(1)}, s16[784,256]{1,0:T(8,128)(2,1)S(1)}, u32[]{:S(2)}, u32[]{:S(2)}) collective-permute-start(s16[784,256]{1,0:T(8,128)(2,1)S(1)} %shard_map.72), channel_id=1, source_target_pairs={{0,4},{1,5},{2,6},{3,7},{4,0},{5,1},{6,2},{7,3},{8,12},{9,13},{10,... | collective-permute-start | bytes 1204232 | tf_op jit(solution)/shard_map/ppermute | solution.py:397
  39.2 10.5 %collective-permute-start.7 = (s16[784,256]{1,0:T(8,128)(2,1)S(1)}, s16[784,256]{1,0:T(8,128)(2,1)S(1)}, u32[]{:S(2)}, u32[]{:S(2)}) collective-permute-start(s16[784,256]{1,0:T(8,128)(2,1)S(1)} %shard_map.74), channel_id=1, source_target_pairs={{0,1},{1,0},{2,3},{3,2},{4,5},{5,4},{6,7},{7,6},{8,9},{9,8},{10,11... | collective-permute-start | bytes 1204232 | tf_op jit(solution)/shard_map/ppermute | solution.py:397
  39.7 10.0 %collective-permute-start.9 = (s16[784,256]{1,0:T(8,128)(2,1)S(1)}, s16[784,256]{1,0:T(8,128)(2,1)S(1)}, u32[]{:S(2)}, u32[]{:S(2)}) collective-permute-start(s16[784,256]{1,0:T(8,128)(2,1)S(1)} %shard_map.76), channel_id=1, source_target_pairs={{0,12},{1,13},{2,14},{3,15},{4,8},{5,9},{6,10},{7,11},{8,4},{9,5},... | collective-permute-start | bytes 1204232 | tf_op jit(solution)/shard_map/ppermute | solution.py:397
  45.5 16.5 %copy-start.5 = (f32[64,64]{1,0:T(8,128)S(1)}, f32[64,64]{1,0:T(8,128)}, u32[]{:S(2)}) copy-start(f32[64,64]{1,0:T(8,128)} %constant.26.clone.table) | copy-start | bytes 49156
  45.5 16.5 %copy-start.6 = (s32[512]{0:T(512)S(1)}, s32[512]{0:T(512)}, u32[]{:S(2)}) copy-start(s32[512]{0:T(512)} %param.8) | copy-start | bytes 6148
  45.5 19.8 %copy-start.4 = (f32[1,192,512]{2,1,0:T(8,128)S(1)}, f32[1,192,512]{2,1,0:T(8,128)}, u32[]{:S(2)}) copy-start(f32[1,192,512]{2,1,0:T(8,128)} %param.7) | copy-start | bytes 1179652
  45.5 7.3 %collective-permute-start.10 = (s16[400,256]{1,0:T(8,128)(2,1)S(1)}, s16[400,256]{1,0:T(8,128)(2,1)S(1)}, u32[]{:S(2)}, u32[]{:S(2)}) collective-permute-start(s16[400,256]{1,0:T(8,128)(2,1)S(1)} %get-tuple-element.35), channel_id=1, source_target_pairs={{0,12},{1,13},{2,14},{3,15},{4,8},{5,9},{6,10},{7,11},{8,4},{9,5},... | collective-permute-start | bytes 614408 | tf_op jit(solution)/shard_map/ppermute | solution.py:397
  50.1 4.7 %collective-permute-start.11 = (s16[400,256]{1,0:T(8,128)(2,1)S(1)}, s16[400,256]{1,0:T(8,128)(2,1)S(1)}, u32[]{:S(2)}, u32[]{:S(2)}) collective-permute-start(s16[400,256]{1,0:T(8,128)(2,1)S(1)} %get-tuple-element.36), channel_id=1, source_target_pairs={{0,4},{1,5},{2,6},{3,7},{4,0},{5,1},{6,2},{7,3},{8,12},{9,13},{10,... | collective-permute-start | bytes 614408 | tf_op jit(solution)/shard_map/ppermute | solution.py:397
  55.0 10.3 %collective-permute-start.12 = (s16[208,512]{1,0:T(8,128)(2,1)S(1)}, s16[208,512]{1,0:T(8,128)(2,1)S(1)}, u32[]{:S(2)}, u32[]{:S(2)}) collective-permute-start(s16[208,512]{1,0:T(8,128)(2,1)S(1)} %get-tuple-element.38), channel_id=1, source_target_pairs={{0,16},{1,17},{2,18},{3,19},{4,20},{5,21},{6,22},{7,23},{8,24},{9,... | collective-permute-start | bytes 638984 | tf_op jit(solution)/shard_map/ppermute | solution.py:449
  66.7 6.8 %collective-permute-start.13 = (f32[24,512]{1,0:T(8,128)S(1)}, f32[24,512]{1,0:T(8,128)S(1)}, u32[]{:S(2)}, u32[]{:S(2)}) collective-permute-start(f32[24,512]{1,0:T(8,128)S(1)} %get-tuple-element.42.kept), channel_id=1, source_target_pairs={{0,32},{32,0},{64,96},{96,64},{128,160},{160,128},{192,224},{224,1... | collective-permute-start | bytes 147464 | tf_op jit(solution)/shard_map/ppermute | solution.py:459
  73.6 3.4 %collective-permute-start.14 = (f32[24,512]{1,0:T(8,128)S(1)}, f32[24,512]{1,0:T(8,128)S(1)}, u32[]{:S(2)}, u32[]{:S(2)}) collective-permute-start(f32[24,512]{1,0:T(8,128)S(1)} %add.18), channel_id=1, source_target_pairs={{0,64},{32,96},{64,0},{96,32},{128,192},{160,224},{192,128},{224,1... | collective-permute-start | bytes 147464 | tf_op jit(solution)/shard_map/ppermute | solution.py:459
  77.0 5.2 %collective-permute-start.15 = (f32[24,512]{1,0:T(8,128)S(1)}, f32[24,512]{1,0:T(8,128)S(1)}, u32[]{:S(2)}, u32[]{:S(2)}) collective-permute-start(f32[24,512]{1,0:T(8,128)S(1)} %add.19), channel_id=1, source_target_pairs={{0,128},{32,160},{64,192},{96,224},{128,0},{160,32},{192,64},{224,... | collective-permute-start | bytes 147464 | tf_op jit(solution)/shard_map/ppermute | solution.py:459
